TPU v7x, 32 devices: a whole 2x2x4 slice. The times are simulated.
32 devices in a mesh: replica: 8 (over y, x, core), tensor: 4 (over z).
Axes of the slice: x: 2, y: 2, z: 4, core: 2. Of those that a mesh axis runs over, the one named last changes fastest.
Arguments:
- queries: bfloat16 [8, 128, 2, 8192], P('replica', None, None, 'tensor'), may hold values from -110 to 110
- step_key_value: bfloat16 [8, 128, 2, 2, 1024], P('replica', None, None, None, 'tensor'), may hold values from -4.1 to 4.1
- replica_page_store: bfloat16 [8, 2, 128, 64, 1024], P('replica', None, None, None, 'tensor'), may hold values from -4 to 4
- page_table: int32 [8, 128, 16], P('replica'), may hold values from 0 to 127
- lengths: int32 [8, 128], P('replica'), may hold values from 1 to 1024, 81920 in all within a row
- mig_offset: int32 [8, 14, 1], P('replica'), may hold values from 0 to 6; in each aligned block of 14 rows (0 to 13, 14 to 27, ..., all dimensions but the last counted through in order) at most 2 rows name the same one
- copy_order: int32 [8, 14, 16], P('replica'), may hold values from 0 to 15, each once within a row
- out_weight: bfloat16 [8192, 8192], P('tensor'), may hold values from -0.0625 to 0.0625
Outputs:
- attention: bfloat16 [8, 128, 2, 8192], P('replica', None, None, 'tensor')
- projected: bfloat16 [8, 128, 2, 8192], P('replica', 'tensor')
- arrived: bfloat16 [8, 14, 4, 2, 64, 1024], P('replica', None, None, None, None, 'tensor')
Inputs may be any that keep to these rules, and one draw needn't show every extreme that they name: Row 114 + j of replica r arrived from replica (r + 1 + mig_offset[r, j, 0]) mod 8; at most 2 of one replica's arriving rows come from one source. `page_table`: entries name pages of the pool of the row's home replica; pages may be shared. `lengths`: each replica has a row of exactly 1024 tokens. `copy_order`: each row is an ordering of its 16 pages.
All inputs are finite; a program needn't handle non-finite values.
Results may differ from a plain program's by a relative error of at most 0.019.
Values may be sent and summed in bfloat16 or wider, within the bound.
A program may use at most 448 MiB of HBM per device.

v0:
```python
import math

import jax
import jax.numpy as jnp
from jax import lax
from jax.sharding import PartitionSpec as P

HEAD_SIZE = 128
MIGRANTS = 14
COPIED = 4


NEG_FILL = -1e30


def attend(query_head_vectors, keys_in, values_in, allowed):
    scores = jnp.einsum(
        "nsgjd,nkgd->nsgjk", query_head_vectors, keys_in, preferred_element_type=jnp.float32
    )
    scores = scores / math.sqrt(query_head_vectors.shape[-1])
    wide_mask = allowed[:, :, None, None, :]
    masked = jnp.where(wide_mask, scores, NEG_FILL)
    highest = jnp.max(masked, axis=-1)
    weights = jnp.where(wide_mask, jnp.exp(masked - highest[..., None]), 0.0).astype(jnp.bfloat16)
    total = jnp.sum(weights.astype(jnp.float32), axis=-1)
    weighted = jnp.einsum(
        "nsgjk,nkgd->nsgjd", weights, values_in, preferred_element_type=jnp.float32
    )
    return (highest, total, weighted)


def merge_parts(first, second):
    highest = jnp.maximum(first[0], second[0])
    scale_first = jnp.exp(first[0] - highest)
    scale_second = jnp.exp(second[0] - highest)
    total = first[1] * scale_first + second[1] * scale_second
    weighted = first[2] * scale_first[..., None] + second[2] * scale_second[..., None]
    return (highest, total, weighted)


def page_rows(pages_local, page_ids, kv_heads):
    selected_pages = jnp.take(pages_local, page_ids, axis=1)
    shape_out = page_ids.shape[:-1] + (
        page_ids.shape[-1] * pages_local.shape[2],
        kv_heads,
        HEAD_SIZE,
    )
    return (selected_pages[0].reshape(shape_out), selected_pages[1].reshape(shape_out))


def page_positions(logical, page_len):
    offsets = lax.broadcasted_iota(jnp.int32, logical.shape + (page_len,), logical.ndim)
    return (logical[..., None] * page_len + offsets).reshape(logical.shape[:-1] + (-1,))


def visible(position, limit):
    seen_once = position < limit[:, None]
    return jnp.broadcast_to(seen_once[:, None, :], (seen_once.shape[0], 2, seen_once.shape[1]))


def pick_slots(received, slot_of):
    count = received.shape[0] * received.shape[1]
    return received.reshape((count,) + received.shape[2:])[slot_of]


def outgoing_pages(pages_local, got_table, logical):
    page_ids = jnp.take_along_axis(got_table, logical, axis=2)
    return jnp.moveaxis(jnp.take(pages_local, page_ids, axis=1), 0, 3)


def body(
    queries,
    step_key_value,
    replica_page_store,
    page_table,
    lengths,
    mig_offset,
    copy_order,
    out_weight,
):
    replicas = lax.axis_size("replica")
    own_index = lax.axis_index("replica")
    capacity = max(2, (MIGRANTS + replicas - 2) // (replicas - 1))
    row_count = queries.shape[1]
    kv_heads = step_key_value.shape[-1] // HEAD_SIZE
    query_group_size = queries.shape[-1] // HEAD_SIZE // kv_heads
    staying = row_count - MIGRANTS
    page_len = replica_page_store.shape[3]
    pages_local = replica_page_store[0]
    row_table = page_table[0]
    row_length = lengths[0]
    query_head_vectors = queries[0].reshape(row_count, 2, kv_heads, query_group_size, HEAD_SIZE)
    fresh_token = step_key_value[0].reshape(row_count, 2, 2, kv_heads, HEAD_SIZE)
    causal = lax.broadcasted_iota(jnp.int32, (2, 2), 1) <= lax.broadcasted_iota(
        jnp.int32, (2, 2), 0
    )
    fresh_part = attend(
        query_head_vectors,
        fresh_token[:, :, 0],
        fresh_token[:, :, 1],
        jnp.broadcast_to(causal, (row_count, 2, 2)),
    )
    source_of = (own_index + 1 + mig_offset[0, :, 0]) % replicas
    earlier = lax.broadcasted_iota(jnp.int32, (MIGRANTS, MIGRANTS), 0) > lax.broadcasted_iota(
        jnp.int32, (MIGRANTS, MIGRANTS), 1
    )
    same_source = source_of[:, None] == source_of[None, :]
    slot_rank = jnp.sum(jnp.where(earlier & same_source, 1, 0), axis=1)
    slot_of = source_of * capacity + slot_rank
    placing = (
        lax.broadcasted_iota(jnp.int32, (replicas * capacity, MIGRANTS), 0) == slot_of[None, :]
    )
    mig_table = row_table[staying:]
    mig_order = copy_order[0]
    mig_length = row_length[staying:]
    send_table = jnp.sum(jnp.where(placing[:, :, None], mig_table[None], 0), axis=1).reshape(
        replicas, capacity, -1
    )
    send_order = jnp.sum(jnp.where(placing[:, :, None], mig_order[None], 0), axis=1).reshape(
        replicas, capacity, -1
    )
    send_length = jnp.sum(jnp.where(placing, mig_length[None], 0), axis=1).reshape(
        replicas, capacity, 1
    )
    got_table, got_order, got_length = (
        lax.all_to_all(send_table, "replica", split_axis=0, concat_axis=0, tiled=True),
        lax.all_to_all(send_order, "replica", split_axis=0, concat_axis=0, tiled=True),
        lax.all_to_all(send_length, "replica", split_axis=0, concat_axis=0, tiled=True),
    )
    cached_page_keys, cached_page_values = page_rows(pages_local, row_table[:staying], kv_heads)
    context_length = lax.broadcasted_iota(jnp.int32, (staying, cached_page_keys.shape[1]), 1)
    staying_part = attend(
        query_head_vectors[:staying],
        cached_page_keys,
        cached_page_values,
        visible(context_length, row_length[:staying]),
    )
    staying_part = merge_parts(staying_part, tuple((member[:staying] for member in fresh_part)))
    mig_queries = query_head_vectors[staying:]
    mig_fresh = tuple((member[staying:] for member in fresh_part))
    sending = outgoing_pages(pages_local, got_table, got_order)
    incoming = lax.all_to_all(sending, "replica", split_axis=0, concat_axis=0, tiled=True)
    own_pages = pick_slots(incoming, slot_of)
    arrived = own_pages[:, :COPIED]
    moved_keys = own_pages[:, :, 0].reshape(MIGRANTS, -1, kv_heads, HEAD_SIZE)
    moved_values = own_pages[:, :, 1].reshape(MIGRANTS, -1, kv_heads, HEAD_SIZE)
    moved_position = page_positions(mig_order, page_len)
    mig_part = attend(mig_queries, moved_keys, moved_values, visible(moved_position, mig_length))
    mig_part = merge_parts(mig_part, mig_fresh)
    total = jnp.concatenate([staying_part[1], mig_part[1]], axis=0)
    weighted = jnp.concatenate([staying_part[2], mig_part[2]], axis=0)
    attention = (weighted / total[..., None]).astype(jnp.bfloat16).reshape(row_count, 2, -1)
    product = jnp.dot(
        attention.reshape(row_count // lax.axis_size("tensor") * lax.axis_size("tensor") * 2, -1),
        out_weight,
        preferred_element_type=jnp.float32,
    )
    projected = lax.psum_scatter(
        product.reshape(
            row_count // lax.axis_size("tensor") * lax.axis_size("tensor"), 2, -1
        ).astype(jnp.bfloat16),
        "tensor",
        scatter_dimension=0,
        tiled=True,
    )
    return (attention[None], projected[None], arrived[None])


def solution(mesh):
    placed = (
        P("replica", None, None, "tensor"),
        P("replica", None, None, None, "tensor"),
        P("replica", None, None, None, "tensor"),
        P("replica", None, None),
        P("replica", None),
        P("replica", None, None),
        P("replica", None, None),
        P("tensor", None),
    )
    return jax.shard_map(
        body,
        mesh=mesh,
        in_specs=placed,
        out_specs=(
            P("replica", None, None, "tensor"),
            P("replica", "tensor", None, None),
            P("replica", None, None, None, None, "tensor"),
        ),
        check_vma=False,
    )
```

profile of v0, /device:TPU:0, one launch (start us, length us, event | category | flops | bytes accessed | tf_op | source)
XLA Modules:
  0.0 691.5 jit_solution(8658199800358051908)
XLA Ops:
  11.0 5.2 all-to-all-start
  21.7 4.8 fusion.60
  28.0 53.1 %gather_fusion = bf16[1824,2,64,256]{3,2,1,0:T(8,128)(2,1)} fusion(bf16[2,128,64,256]{3,2,1,0:T(8,128)(2,1)} %bitcast.132, s32[2048]{0:T(1024)S(1)} %pad_clamp_fusion), kind=kCustom, calls=%fused_computation | custom fusion | bytes 239082624 | tf_op jit(solution)/shard_map/jit(_take)/gather | solution.py:42
  81.1 77.3 %fusion = bf16[2,114,16,64,256]{4,3,2,1,0:T(8,128)(2,1)} fusion(bf16[114,16,2,64,256]{4,3,2,1,0:T(8,128)(2,1)} %bitcast.3, pred[114,16]{1,0:T(8,128)(4,1)S(1)} %copy.125), kind=kLoop, calls=%fused_computation.5 | loop fusion | flops 59768832 | bytes 239077152 | tf_op jit(solution)/shard_map/jit(_take)/select_n | solution.py:42
  165.7 4.2 all-to-all-start.1
  170.1 4.6 all-to-all-done.1
  174.6 2.7 gather_fusion.3
  177.6 13.2 %gather_fusion.1 = bf16[256,2,64,256]{3,2,1,0:T(8,128)(2,1)} fusion(bf16[2,128,64,256]{3,2,1,0:T(8,128)(2,1)} %bitcast.133, s32[1024]{0:T(1024)S(1)} %pad_clamp_fusion.2), kind=kCustom, calls=%fused_computation.1 | custom fusion | bytes 33555456 | tf_op jit(solution)/shard_map/jit(_take)/gather | solution.py:68
  190.8 14.1 %broadcast_select_fusion = bf16[8,2,16,2,64,256]{5,4,3,2,1,0:T(8,128)(2,1)} fusion(bf16[8,2,16,2,64,256]{5,4,3,2,1,0:T(8,128)(2,1)} %bitcast.134, pred[8,2,16]{2,1,0:T(4,128)(4,1)S(1)} %get-tuple-element.29), kind=kLoop, calls=%fused_computation.12 | loop fusion | flops 8388608 | bytes 33554688 | tf_op jit(solution)/shard_map/jit(_take)/select_n | solution.py:68
  204.9 5.7 all-to-all-start.2
  210.8 77.6 %fusion.57 = (bf16[1,114,16,64,256]{4,3,2,1,0:T(8,128)(2,1)}, bf16[1,114,16,64,256]{4,3,2,1,0:T(8,128)(2,1)}) fusion(bf16[2,114,16,64,256]{4,3,2,1,0:T(8,128)(2,1)} %fusion), kind=kLoop, calls=%fused_computation.104 | loop fusion | bytes 239075328 | tf_op jit(solution)/shard_map/slice | solution.py:48
  288.4 81.0 %reshape_squeeze.18 = bf16[114,1024,2,128]{3,2,1,0:T(2,128)(2,1)} reshape(bf16[1,114,16,64,256]{4,3,2,1,0:T(8,128)(2,1)} %get-tuple-element.33) | data formatting | bytes 119537664 | tf_op jit(solution)/shard_map/reshape;squeeze | solution.py:48
  369.5 81.1 %reshape_squeeze.19 = bf16[114,1024,2,128]{3,2,1,0:T(2,128)(2,1)} reshape(bf16[1,114,16,64,256]{4,3,2,1,0:T(8,128)(2,1)} %get-tuple-element.34) | data formatting | bytes 119537664 | tf_op jit(solution)/shard_map/reshape;squeeze | solution.py:48
  450.8 31.2 %bitcast_reduce_fusion = (f32[114,2,2,8]{3,1,2,0:T(2,128)S(1)}, f32[114,2,1024,2,8]{2,4,3,1,0:T(8,128)}) fusion(pred[114,1024]{1,0:T(8,128)(4,1)S(1)} %iota_compare_fusion, bf16[114,2,2,8,128]{4,3,2,1,0:T(8,128)(2,1)S(1)} %copy-done.1, bf16[114,1024,2,128,1]{3,2,1,0,4:T(2,128)(2,1)} %bitcast.136), kind=kOutput, calls=%fused_computation.14 | convolution fusion | flops 967504320 | bytes 75776256 | tf_op jit(solution)/shard_map/nsgjd,nkgd->nsgjk/dot_general | solution.py:17
  482.1 8.4 %convert_reduce_fusion = f32[114,2,2,8]{3,1,2,0:T(2,128)S(1)} fusion(f32[114,2,2,8]{3,1,2,0:T(2,128)S(1)} %get-tuple-element.43, f32[114,2,1024,2,8]{2,4,3,1,0:T(8,128)} %get-tuple-element.44, pred[114,1024]{1,0:T(8,128)(4,1)S(1)} %iota_compare_fusion), kind=kLoop, calls=%fused_computation.18 | loop fusion | flops 26145216 | bytes 15088128 | tf_op jit(solution)/shard_map/reduce_sum | solution.py:25
  491.3 1.8 convolution_bitcast_fusion
  493.2 28.9 %fusion.19 = f32[114,2,2,8,128]{4,3,1,2,0:T(8,128)S(1)} fusion(f32[128,2,2,8,128]{4,3,1,2,0:T(8,128)} %convolution_bitcast_fusion, bf16[114,1024,2,128,1]{3,2,1,0,4:T(2,128)(2,1)} %bitcast.135, f32[114,2,2,8]{3,1,2,0:T(2,128)S(1)} %copy.140, f32[114,2,2,8]{3,1,2,0:T(2,128)S(1)} %copy.138, f32[114,2,1024,2,8]{2,4,3,1,0:T(8,128)} %get-tuple-element.44, ...), kind=kOutput, calls=%fused_computation.31 | convolution fusion | flops 976379904 | bytes 79392768 | tf_op jit(solution)/shard_map/nsgjk,nkgd->nsgjd/dot_general | solution.py:26
  522.1 12.5 %gather_fusion.2 = bf16[14,16,2,64,256]{4,3,2,1,0:T(8,128)(2,1)} fusion(bf16[16,16,2,64,256]{4,3,2,1,0:T(8,128)(2,1)} %bitcast.25, s32[1024]{0:T(1024)S(1)} %pad_clamp_fusion.1), kind=kCustom, calls=%fused_computation.2 | custom fusion | bytes 29360184 | tf_op jit(solution)/shard_map/gather | solution.py:63
  534.6 10.8 %fusion.58 = (bf16[14,16,1,64,256]{4,3,2,1,0:T(8,128)(2,1)}, bf16[14,16,1,64,256]{4,3,2,1,0:T(8,128)(2,1)}) fusion(bf16[14,16,2,64,256]{4,3,2,1,0:T(8,128)(2,1)} %gather_fusion.2), kind=kLoop, calls=%fused_computation.105 | loop fusion | bytes 29360128 | tf_op jit(solution)/shard_map/slice | solution.py:146
  545.4 11.1 %reshape_squeeze.22 = bf16[14,1024,2,128]{3,2,1,0:T(2,128)(2,1)} reshape(bf16[14,16,1,64,256]{4,3,2,1,0:T(8,128)(2,1)} %get-tuple-element.35) | data formatting | bytes 14680064 | tf_op jit(solution)/shard_map/reshape;squeeze | solution.py:146
  556.5 11.1 %reshape_squeeze.23 = bf16[14,1024,2,128]{3,2,1,0:T(2,128)(2,1)} reshape(bf16[14,16,1,64,256]{4,3,2,1,0:T(8,128)(2,1)} %get-tuple-element.36) | data formatting | bytes 14680064 | tf_op jit(solution)/shard_map/reshape;squeeze | solution.py:145
  567.7 6.4 bitcast_reduce_fusion.1
  574.2 2.2 convert_reduce_fusion.1
  577.0 5.1 fusion.33
  583.7 1.9 copy.160
  585.6 16.8 %fusion.10 = bf16[128,2,8192]{2,0,1:T(8,128)(2,1)} fusion(bf16[128,2,2048]{0,2,1:T(8,128)(2,1)S(1)} %bitcast.140, bf16[2048,8192]{1,0:T(8,128)(2,1)} %param.15), kind=kOutput, calls=%fused_computation.20 | convolution fusion | flops 8592031744 | bytes 38797312 | tf_op jit(solution)/shard_map/dot_general | solution.py:153
  603.8 3.0 concatenate.19
  608.9 3.3 fusion.17
  612.2 2.0 copy.162
  614.2 4.4 slice_bitcast_fusion
  618.6 62.3 %reduce-scatter.2.cloned.1.call-done = bf16[32,2,8192]{2,0,1:T(8,128)(2,1)} async-done(((bf16[128,2,8192]{2,0,1:T(8,128)(2,1)}), bf16[32,2,8192]{2,0,1:T(8,128)(2,1)}) %reduce-scatter.2.cloned.1.call-update) | async-done | bytes 1048592 | tf_op jit(solution)/shard_map/reduce_scatter | solution.py:158
  680.9 3.3 copy.163
  (102 shorter events, 25.3 us)
Async XLA Ops:
  8.0 1.4 copy-start.11
  11.0 154.7 %all-to-all-start = ((s32[8,2,16]{2,1,0:T(2,128)}), s32[8,2,16]{2,1,0:T(2,128)S(1)}, u32[]{:S(2)}, u32[]{:S(2)}) async-start(s32[8,2,16]{2,1,0:T(2,128)} %bitcast.20), calls=%async_computation | async-start | bytes 16384 | tf_op jit(solution)/shard_map/all_to_all | solution.py:127
  81.1 78.8 %slice-start = ((bf16[1,128,2,2048]{3,2,1,0:T(2,128)(2,1)}), bf16[1,14,2,2048]{3,2,1,0:T(2,128)(2,1)S(1)}, s32[]{:S(2)}) async-start(bf16[1,128,2,2048]{3,2,1,0:T(2,128)(2,1)} %param.8), calls=%async_computation.5 | async-start | bytes 229376 | tf_op jit(solution)/shard_map/slice | solution.py:139
  81.1 80.3 %slice-start.1 = ((bf16[1,128,2,2048]{3,2,1,0:T(2,128)(2,1)}), bf16[1,114,2,2048]{3,2,1,0:T(2,128)(2,1)S(1)}, s32[]{:S(2)}) async-start(bf16[1,128,2,2048]{3,2,1,0:T(2,128)(2,1)} %param.8), calls=%async_computation.6 | async-start | bytes 1867776 | tf_op jit(solution)/shard_map/slice | solution.py:133
  165.7 8.9 %all-to-all-start.1 = ((s32[8,2,16]{2,1,0:T(2,128)}), s32[8,2,16]{2,1,0:T(2,128)S(1)}, u32[]{:S(2)}, u32[]{:S(2)}) async-start(s32[8,2,16]{2,1,0:T(2,128)} %bitcast.22), calls=%async_computation.1 | async-start | bytes 16384 | tf_op jit(solution)/shard_map/all_to_all | solution.py:126
  204.9 317.2 %all-to-all-start.2 = ((bf16[8,2,16,2,64,256]{5,4,3,2,1,0:T(8,128)(2,1)}), bf16[8,2,16,2,64,256]{5,4,3,2,1,0:T(8,128)(2,1)}, u32[]{:S(2)}, u32[]{:S(2)}) async-start(bf16[8,2,16,2,64,256]{5,4,3,2,1,0:T(8,128)(2,1)} %broadcast_select_fusion), calls=%async_computation.2 | async-start | bytes 33554432 | tf_op jit(solution)/shard_map/all_to_all | solution.py:142
  210.6 470.3 %reduce-scatter.2.cloned.1.call-start = ((), (), s32[]{:S(2)}) async-start(), calls=%async_computation.4 | async-start | bytes 5242880 | tf_op jit(solution)/shard_map/reduce_scatter | solution.py:158
  369.5 81.2 %copy-start.13 = (s32[1,128]{1,0:T(1,128)S(1)}, s32[1,128]{1,0:T(1,128)}, u32[]{:S(2)}) copy-start(s32[1,128]{1,0:T(1,128)} %param.12) | copy-start | bytes 1540
  369.5 81.3 %copy-start.1 = (bf16[114,2,2,8,128]{4,3,2,1,0:T(8,128)(2,1)S(1)}, bf16[114,2,2,8,128]{4,3,2,1,0:T(8,128)(2,1)}, u32[]{:S(2)}) copy-start(bf16[114,2,2,8,128]{4,3,2,1,0:T(8,128)(2,1)} %reshape.302) | copy-start | bytes 2801668
  482.1 8.6 %copy-start.7 = (f32[114,2,2,8]{0,3,2,1:T(8,128)S(1)}, f32[114,2,2,8]{0,3,2,1:T(8,128)}, u32[]{:S(2)}) copy-start(f32[114,2,2,8]{0,3,2,1:T(8,128)} %copy.188) | copy-start | bytes 43780
  482.1 8.6 %copy-start.8 = (f32[114,2,2,8]{0,3,2,1:T(8,128)S(1)}, f32[114,2,2,8]{0,3,2,1:T(8,128)}, u32[]{:S(2)}) copy-start(f32[114,2,2,8]{0,3,2,1:T(8,128)} %copy.185) | copy-start | bytes 43780
  482.1 9.0 %copy-start.10 = (s32[1,14,1]{1,2,0:T(1,128)S(1)}, s32[1,14,1]{1,2,0:T(1,128)}, u32[]{:S(2)}) copy-start(s32[1,14,1]{1,2,0:T(1,128)} %param.13) | copy-start | bytes 172
  482.1 9.0 %copy-start.12 = (s32[14]{0:T(128)S(1)}, s32[14]{0:T(128)}, u32[]{:S(2)}) copy-start(s32[14]{0:T(128)} %copy-done.11) | copy-start | bytes 172
  482.1 9.1 %copy-start.3 = (s32[14,1024]{1,0:T(8,128)S(1)}, s32[14,1024]{1,0:T(8,128)}, u32[]{:S(2)}) copy-start(s32[14,1024]{1,0:T(8,128)} %add.169) | copy-start | bytes 172036
  482.1 9.1 %copy-start.9 = (s32[1024]{0:T(1024)S(1)}, s32[1024]{0:T(1024)}, u32[]{:S(2)}) copy-start(s32[1024]{0:T(1024)} %iota.54) | copy-start | bytes 12292
  482.1 9.2 %copy-start = (bf16[128,2,2,8,2]{3,4,1,2,0:T(2,128)(2,1)S(1)}, bf16[128,2,2,8,2]{3,4,1,2,0:T(2,128)(2,1)}, u32[]{:S(2)}) copy-start(bf16[128,2,2,8,2]{3,4,1,2,0:T(2,128)(2,1)} %get-tuple-element.32) | copy-start | bytes 49156
  482.1 9.2 %copy-start.2 = (bf16[128,2,1,2,128]{4,1,3,0,2:T(2,128)(2,1)S(1)}, bf16[128,2,1,2,128]{4,1,3,0,2:T(2,128)(2,1)}, u32[]{:S(2)}) copy-start(bf16[128,2,1,2,128]{4,1,3,0,2:T(2,128)(2,1)} %copy.186) | copy-start | bytes 393220
  556.5 11.1 %copy-start.4 = (bf16[14,2,2,8,128]{4,3,2,1,0:T(8,128)(2,1)S(1)}, bf16[14,2,2,8,128]{4,3,2,1,0:T(8,128)(2,1)}, u32[]{:S(2)}) copy-start(bf16[14,2,2,8,128]{4,3,2,1,0:T(8,128)(2,1)} %slice.88) | copy-start | bytes 344068
  567.7 8.8 %copy-start.5 = (f32[14,2,2,8]{0,3,2,1:T(8,128)S(1)}, f32[14,2,2,8]{0,3,2,1:T(8,128)}, u32[]{:S(2)}) copy-start(f32[14,2,2,8]{0,3,2,1:T(8,128)} %copy.189) | copy-start | bytes 5380
  567.7 8.8 %copy-start.6 = (f32[14,2,2,8]{0,3,2,1:T(8,128)S(1)}, f32[14,2,2,8]{0,3,2,1:T(8,128)}, u32[]{:S(2)}) copy-start(f32[14,2,2,8]{0,3,2,1:T(8,128)} %copy.187) | copy-start | bytes 5380
Sparse Core Ops, SparseCore 0:
  602.5 78.3 reduce-scatter.1
where the time goes:
time: 705 us; the launch traced here: 691 us
  local copies, waits for them, and re-layouts  386 us (55%)
  other arithmetic  113 us (16%)
  matrix products  95.1 us (13%)
  waiting for transfers between devices  66.9 us (9%)
  starting transfers between devices  15.3 us (2%)
  between operations  14.8 us (2%)
    another operation x1, local copies, waits for them, and re-layouts, page_rows(): selected_pages[0].reshape(shape_out)  81.1 us
    another operation x1, local copies, waits for them, and re-layouts, page_rows(): selected_pages[1].reshape(shape_out)  81 us
    select_n x2, other arithmetic, page_rows(): selected_pages = jnp.take(pages_local, page_ids, axis=1)  78 us
    slice x1, local copies, waits for them, and re-layouts, page_rows(): selected_pages[1].reshape(shape_out)  77.6 us
    reduce_scatter x1, waiting for transfers between devices, body(): lax.psum_scatter(product.reshape(row_count // lax.axis_size('tensor') * l...  62.3 us
    gather x1, local copies, waits for them, and re-layouts, page_rows(): selected_pages = jnp.take(pages_local, page_ids, axis=1)  53.1 us
    dot_general x3, matrix products, attend(): jnp.einsum('nsgjd,nkgd->nsgjk', query_head_vectors, keys_in, preferred_el...  42.4 us
    dot_general x3, matrix products, attend(): jnp.einsum('nsgjk,nkgd->nsgjd', weights, values_in, preferred_element_typ...  35.9 us
  transfers between devices with their start and end apart: 4, of which 2 were waited for; matrix products, arithmetic and copies ran while one was open for 69% of the time, Pallas kernels for 0%

commit v1 on v0

v1 whole, which is shorter than its diff:
```python
import functools
import math

import jax
import jax.numpy as jnp
from jax import lax
from jax.experimental import pallas as pl
from jax.experimental.pallas import tpu as pltpu
from jax.sharding import PartitionSpec as P

HEAD_SIZE = 128
MIGRANTS = 14
COPIED = 4
CHUNKS = 4
NEG_FILL = -1e30


def attend_rows(rows, kv_heads, group, pages, page_len, table, lengths, queries, fresh, pool, out):
    context = pages * page_len
    scale = math.log2(math.e) / math.sqrt(HEAD_SIZE)
    height = kv_heads * 2 * group
    position = lax.broadcasted_iota(jnp.int32, (1, context), 1)
    step = lax.broadcasted_iota(jnp.int32, (height, 1), 0) // group % 2
    scores, news = [], []
    for row in rows:
        q = queries[0, row]
        keys = jnp.concatenate([pool[0, 0, table[row, i]] for i in range(pages)], axis=0)
        scores.append(
            lax.dot_general(q, keys, (((1,), (1,)), ((), ())), preferred_element_type=jnp.float32)
        )
        wide = q.astype(jnp.float32)
        token = fresh[0, row]
        first = jnp.sum(wide * token[0:1], axis=1, keepdims=True) * scale
        second = jnp.sum(wide * token[2:3], axis=1, keepdims=True) * scale
        news.append((first, jnp.where(step > 0, second, NEG_FILL)))
    parts = []
    for row, s, (first, second) in zip(rows, scores, news):
        s = jnp.where(position < lengths[row], s * scale, NEG_FILL)
        highest = jnp.maximum(jnp.max(s, axis=1, keepdims=True), jnp.maximum(first, second))
        weights = jnp.exp2(s - highest)
        first = jnp.exp2(first - highest)
        second = jnp.exp2(second - highest)
        total = jnp.sum(weights, axis=1, keepdims=True) + first + second
        parts.append((weights.astype(jnp.bfloat16), first, second, total))
    for row, (weights, first, second, total) in zip(rows, parts):
        values = jnp.concatenate([pool[0, 1, table[row, i]] for i in range(pages)], axis=0)
        weighted = jnp.dot(weights, values, preferred_element_type=jnp.float32)
        token = fresh[0, row]
        weighted = weighted + first * token[1:2] + second * token[3:4]
        weighted = weighted / total
        for g in range(kv_heads):
            block = weighted[g * 2 * group : (g + 1) * 2 * group, g * HEAD_SIZE : (g + 1) * HEAD_SIZE]
            out[row, g * 2 * group : (g + 1) * 2 * group] = block.astype(jnp.bfloat16)


def chunk_kernel(
    sizes, unroll, row_of, staying, table, lengths, queries, fresh, pool, out
):
    def step(index, carry):
        base = index * unroll

        @pl.when(row_of(base) < staying)
        def _():
            attend_rows(
                [base + k for k in range(unroll)], *sizes, table, lengths, queries, fresh, pool, out
            )

        return carry

    lax.fori_loop(0, out.shape[0] // unroll, step, 0)


def slot_kernel(sizes, unroll, table, lengths, wanted, queries, fresh, pool, out, copied):
    def copy(row, carry):
        for c in range(COPIED):
            copied[row, c, 0] = pool[0, 0, wanted[row, c]]
            copied[row, c, 1] = pool[0, 1, wanted[row, c]]
        return carry

    lax.fori_loop(0, out.shape[0], copy, 0)

    def step(index, carry):
        attend_rows(
            [index * unroll + k for k in range(unroll)],
            *sizes, table, lengths, queries, fresh, pool, out
        )
        return carry

    lax.fori_loop(0, out.shape[0] // unroll, step, 0)


def unroll_of(count):
    return next(u for u in (4, 2, 1) if count % u == 0)


def body(
    queries,
    step_key_value,
    replica_page_store,
    page_table,
    lengths,
    mig_offset,
    copy_order,
    out_weight,
):
    replicas = lax.axis_size("replica")
    shards = lax.axis_size("tensor")
    own_index = lax.axis_index("replica")
    capacity = max(2, (MIGRANTS + replicas - 2) // (replicas - 1))
    slots = replicas * capacity
    row_count = queries.shape[1]
    width = queries.shape[-1]
    kv_width = step_key_value.shape[-1]
    kv_heads = kv_width // HEAD_SIZE
    group = width // HEAD_SIZE // kv_heads
    height = kv_heads * 2 * group
    staying = row_count - MIGRANTS
    pages = page_table.shape[-1]
    page_len = replica_page_store.shape[3]
    per_shard = row_count // shards
    share = per_shard // CHUNKS
    chunk_rows = share * shards
    sizes = (kv_heads, group, pages, page_len)

    def spread(q):
        q = q.reshape(-1, 2, kv_heads, group, HEAD_SIZE).transpose(0, 2, 1, 3, 4)
        same = jnp.eye(kv_heads, dtype=jnp.bool_)[None, :, None, None, :, None]
        q = jnp.where(same, q[:, :, :, :, None, :], jnp.zeros((), q.dtype))
        return q.reshape(-1, height, kv_width)

    def gathered(att):
        att = att.reshape(-1, kv_heads, 2, group, HEAD_SIZE).transpose(0, 2, 1, 3, 4)
        return att.reshape(-1, 2, width)

    def by_chunk(x):
        x = x.reshape((shards, CHUNKS, share) + x.shape[1:])
        x = jnp.moveaxis(x, 1, 0)
        return x.reshape((CHUNKS, chunk_rows) + x.shape[3:])

    source_of = (own_index + 1 + mig_offset[0, :, 0]) % replicas
    earlier = lax.broadcasted_iota(jnp.int32, (MIGRANTS, MIGRANTS), 0) > lax.broadcasted_iota(
        jnp.int32, (MIGRANTS, MIGRANTS), 1
    )
    same_source = source_of[:, None] == source_of[None, :]
    slot_rank = jnp.sum(jnp.where(earlier & same_source, 1, 0), axis=1)
    slot_of = source_of * capacity + slot_rank
    placing = lax.broadcasted_iota(jnp.int32, (slots, MIGRANTS), 0) == slot_of[None, :]
    mig_table = page_table[0, staying:]
    mig_wanted = jnp.take_along_axis(mig_table, copy_order[0, :, :COPIED], axis=1)
    mig_ints = jnp.concatenate(
        [mig_table, mig_wanted, lengths[0, staying:, None]], axis=1
    )
    send_ints = jnp.sum(jnp.where(placing[:, :, None], mig_ints[None], 0), axis=1)
    mig_rows = jnp.concatenate(
        [
            queries[0, staying:].reshape(MIGRANTS, -1),
            step_key_value[0, staying:].reshape(MIGRANTS, -1),
        ],
        axis=1,
    )
    place = placing.astype(jnp.bfloat16)
    send_rows = jnp.dot(place, mig_rows, preferred_element_type=jnp.float32).astype(jnp.bfloat16)
    got_ints = lax.all_to_all(
        send_ints.reshape(replicas, capacity, -1), "replica", 0, 0, tiled=True
    ).reshape(slots, -1)
    got_rows = lax.all_to_all(
        send_rows.reshape(replicas, capacity, -1), "replica", 0, 0, tiled=True
    ).reshape(slots, -1)

    smem = pl.BlockSpec(memory_space=pltpu.SMEM)
    vmem = pl.BlockSpec(memory_space=pltpu.VMEM)
    params = pltpu.CompilerParams(vmem_limit_bytes=40 * 2**20)

    slot_cost = pl.CostEstimate(
        flops=4 * slots * height * pages * page_len * kv_width,
        bytes_accessed=12 * 2**20,
        transcendentals=slots * height * pages * page_len,
    )
    slot_att, sending = pl.pallas_call(
        functools.partial(slot_kernel, sizes, unroll_of(slots)),
        out_shape=(
            jax.ShapeDtypeStruct((slots, height, HEAD_SIZE), jnp.bfloat16),
            jax.ShapeDtypeStruct((slots, COPIED, 2, page_len, kv_width), jnp.bfloat16),
        ),
        in_specs=[smem, smem, smem, vmem, vmem, vmem],
        out_specs=(vmem, vmem),
        compiler_params=params,
        cost_estimate=slot_cost,
        name="slot_attention",
    )(
        got_ints[:, :pages],
        got_ints[:, pages + COPIED],
        got_ints[:, pages : pages + COPIED],
        spread(got_rows[:, : 2 * width].reshape(slots, 2, width))[None],
        got_rows[:, 2 * width :].astype(jnp.float32).reshape(1, slots, 4, kv_width),
        replica_page_store,
    )
    incoming = lax.all_to_all(
        sending.reshape((replicas, capacity) + sending.shape[1:]), "replica", 0, 0, tiled=True
    ).reshape(sending.shape)
    arrived = jnp.take(incoming, slot_of, axis=0, mode="clip")
    back = lax.all_to_all(
        gathered(slot_att).reshape(replicas, capacity, -1), "replica", 0, 0, tiled=True
    ).reshape(slots, -1)
    mig_att = (
        jnp.dot(place.T, back, preferred_element_type=jnp.float32)
        .astype(jnp.bfloat16)
        .reshape(MIGRANTS, 2, width)
    )

    all_queries = by_chunk(spread(queries[0]))
    all_fresh = by_chunk(step_key_value[0].astype(jnp.float32).reshape(row_count, 4, kv_width))
    all_table = by_chunk(page_table[0])
    all_lengths = by_chunk(lengths[0])
    chunk_cost = pl.CostEstimate(
        flops=4 * chunk_rows * height * pages * page_len * kv_width,
        bytes_accessed=9 * 2**20,
        transcendentals=chunk_rows * height * pages * page_len,
    )
    unroll = unroll_of(share)
    attention, projected = [], []
    for c in range(CHUNKS):

        def row_of(j, c=c):
            return j // share * per_shard + c * share + j % share

        att = pl.pallas_call(
            functools.partial(chunk_kernel, sizes, unroll, row_of, staying),
            grid=(1,),
            out_shape=jax.ShapeDtypeStruct((chunk_rows, height, HEAD_SIZE), jnp.bfloat16),
            in_specs=[
                smem,
                smem,
                pl.BlockSpec((1, chunk_rows, height, kv_width), lambda i, c=c: (c, 0, 0, 0)),
                pl.BlockSpec((1, chunk_rows, 4, kv_width), lambda i, c=c: (c, 0, 0, 0)),
                vmem,
            ],
            out_specs=vmem,
            compiler_params=params,
            cost_estimate=chunk_cost,
            name="chunk_attention",
        )(all_table[c], all_lengths[c], all_queries, all_fresh, replica_page_store)
        att = gathered(att)
        for t in range(shards):
            low = t * per_shard + c * share
            first = max(low, staying)
            if first < low + share:
                at = t * share + first - low
                piece = mig_att[first - staying : low + share - staying]
                att = lax.dynamic_update_slice(att, piece, (at, 0, 0))
        attention.append(att)
        product = jnp.dot(
            att.reshape(chunk_rows * 2, width), out_weight, preferred_element_type=jnp.float32
        ).astype(jnp.bfloat16)
        if projected:
            product, projected[-1] = lax.optimization_barrier((product, projected[-1]))
        projected.append(lax.psum_scatter(product, "tensor", scatter_dimension=0, tiled=True))
    attention = jnp.stack([a.reshape(shards, share, 2, width) for a in attention], axis=1)
    attention = attention.reshape(1, row_count, 2, width)
    projected = jnp.concatenate(projected, axis=0).reshape(per_shard, 2, -1)
    return (attention, projected[None], arrived[None])


def solution(mesh):
    placed = (
        P("replica", None, None, "tensor"),
        P("replica", None, None, None, "tensor"),
        P("replica", None, None, None, "tensor"),
        P("replica", None, None),
        P("replica", None),
        P("replica", None, None),
        P("replica", None, None),
        P("tensor", None),
    )
    return jax.shard_map(
        body,
        mesh=mesh,
        in_specs=placed,
        out_specs=(
            P("replica", None, None, "tensor"),
            P("replica", "tensor", None, None),
            P("replica", None, None, None, None, "tensor"),
        ),
        check_vma=False,
    )
```

time: 705 us -> 235 us (0.33); the launches traced: 691 us -> 234 us
  local copies, waits for them, and re-layouts: 386 us -> 46 us
  other arithmetic: 113 us -> 4.96 us
  Pallas kernels: 0 us -> 40.7 us
  matrix products: 95.1 us -> 59.6 us
  waiting for transfers between devices: 66.9 us -> 50.2 us
    another operation x5 -> x12, local copies, waits for them, and re-layouts: 186 us -> 6.42 us  [the longest x2 1.92 us: spread(): q = q.reshape(-1, 2, kv_heads, group, HEAD_SIZE).transpose(0, 2, 1, 3, 4)]
    select_n x4 -> x2, other arithmetic: 92.1 us -> 0.03 us  [the longest x1 0.02 us: spread(): q = jnp.where(same, q[:, :, :, :, None, :], jnp.zeros((), q.dtype))]
    slice x13 -> x8, local copies, waits for them, and re-layouts: 90.7 us -> 1.11 us  [the longest x1 0.78 us: body(): copy_order[0, :, :COPIED]]
    gather x6, local copies, waits for them, and re-layouts: 81.7 us -> 6.24 us  [the longest x1 4.93 us: body(): arrived = jnp.take(incoming, slot_of, axis=0, mode='clip')]
    pallas_call x0 -> x5, Pallas kernels: none -> 40.7 us  [the longest x4 35.2 us: body(): pl.pallas_call(functools.partial(chunk_kernel, sizes, unroll, row_of, sta...]
    dot_general x7 -> x6, matrix products: 95.1 us -> 59.6 us  [the longest x4 59.1 us: body(): jnp.dot(att.reshape(chunk_rows * 2, width), out_weight, preferred_element...]
    reduce_scatter x1 -> x4, waiting for transfers between devices: 62.3 us -> 50.1 us  [body(): lax.psum_scatter(product, 'tensor', scatter_dimension=0, tiled=True)]
    reduce_sum x4 -> x1, other arithmetic: 12.8 us -> 0.7 us  [body(): jnp.sum(jnp.where(placing[:, :, None], mig_ints[None], 0), axis=1)]
  transfers between devices with their start and end apart: 4 -> 8, of which waited for: 2 -> 3; matrix products, arithmetic and copies ran while one was open for 69% -> 36% of each run, Pallas kernels for 0% -> 17%
where the time goes in v1:
time: 235 us; the launch traced here: 234 us
  matrix products  59.6 us (25%)
  waiting for transfers between devices  50.2 us (21%)
  local copies, waits for them, and re-layouts  46 us (20%)
  Pallas kernels  40.7 us (17%)
  starting transfers between devices  18.2 us (8%)
  between operations  14.3 us (6%)
  other arithmetic  4.96 us (2%)
    dot_general x4, matrix products, body(): jnp.dot(att.reshape(chunk_rows * 2, width), out_weight, preferred_element...  59.1 us
    reduce_scatter x4, waiting for transfers between devices, body(): lax.psum_scatter(product, 'tensor', scatter_dimension=0, tiled=True)  50.1 us
    pallas_call x4, Pallas kernels, body(): pl.pallas_call(functools.partial(chunk_kernel, sizes, unroll, row_of, sta...  35.2 us
    unnamed x34, local copies, waits for them, and re-layouts  22.7 us
    pallas_call x1, Pallas kernels, body(): pl.pallas_call(functools.partial(slot_kernel, sizes, unroll_of(slots)), o...  5.55 us
    all_to_all x1, starting transfers between devices, body(): lax.all_to_all(send_ints.reshape(replicas, capacity, -1), 'replica', 0, 0...  5.17 us
    gather x1, local copies, waits for them, and re-layouts, body(): arrived = jnp.take(incoming, slot_of, axis=0, mode='clip')  4.93 us
  transfers between devices with their start and end apart: 8, of which 3 were waited for; matrix products, arithmetic and copies ran while one was open for 36% of the time, Pallas kernels for 17%

profile of v1, /device:TPU:0, one launch (start us, length us, event | category | flops | bytes accessed | tf_op | source)
XLA Modules:
  0.0 234.0 jit_solution(15057189397789948456)
XLA Ops:
  13.2 5.2 %all-to-all-start = ((s32[8,2,21]{2,1,0:T(2,128)}), s32[8,2,21]{2,1,0:T(2,128)S(1)}, u32[]{:S(2)}, u32[]{:S(2)}) async-start(s32[8,2,21]{2,1,0:T(2,128)} %bitcast.28), calls=%async_computation | async-start | bytes 16384 | tf_op jit(solution)/shard_map/all_to_all | solution.py:163
  20.2 1.7 reshape_squeeze.17
  22.9 3.4 %copy-done = bf16[1,2,128,64,256]{4,3,2,1,0:T(8,128)(2,1)S(1)} copy-done((bf16[1,2,128,64,256]{4,3,2,1,0:T(8,128)(2,1)S(1)}, bf16[1,2,128,64,256]{4,3,2,1,0:T(8,128)(2,1)}, u32[]{:S(2)}) %copy-start) | copy-done | bytes 8388632
  26.3 9.6 %chunk_attention.4 = bf16[32,32,128]{2,1,0:T(8,128)(2,1)S(1)} custom-call(s32[32,16]{1,0:T(8,128)S(1)} %get-tuple-element.29.table, s32[32]{0:T(128)S(1)} %squeeze.38.lengths, bf16[4,32,32,256]{3,2,1,0:T(8,128)(2,1)S(1)} %bitcast.128, f32[4,32,4,256]{3,2,1,0:T(4,128)S(1)} %bitcast.132, bf16[1,2,128,64,256]{4,3,2,1,0:T(8,128)(2,1)S(1)} %copy-done), custom_call_target="tpu_custom_call" | custom-call | flops 1073741824 | bytes 9437184 | tf_op jit(solution)/shard_map/chunk_attention/pallas_call | solution.py:227
  36.1 14.6 %convolution_convert_fusion.2 = bf16[64,8192]{1,0:T(8,128)(2,1)} fusion(bf16[64,2048]{1,0:T(8,128)(2,1)S(1)} %reshape_reshape.17, bf16[2048,8192]{1,0:T(8,128)(2,1)} %param.15), kind=kOutput, calls=%fused_computation.4 | convolution fusion | flops 2148007936 | bytes 34865152 | tf_op jit(solution)/shard_map/dot_general | solution.py:252
  50.8 1.0 slice_bitcast_fusion.1
  52.3 3.4 %copy-done.1 = bf16[1,2,128,64,256]{4,3,2,1,0:T(8,128)(2,1)S(1)} copy-done((bf16[1,2,128,64,256]{4,3,2,1,0:T(8,128)(2,1)S(1)}, bf16[1,2,128,64,256]{4,3,2,1,0:T(8,128)(2,1)}, u32[]{:S(2)}) %copy-start.1) | copy-done | bytes 8388632
  55.7 9.6 %chunk_attention.5 = bf16[32,32,128]{2,1,0:T(8,128)(2,1)S(1)} custom-call(s32[32,16]{1,0:T(8,128)S(1)} %get-tuple-element.32.table, s32[32]{0:T(128)S(1)} %squeeze.40.lengths, bf16[4,32,32,256]{3,2,1,0:T(8,128)(2,1)S(1)} %bitcast.129, f32[4,32,4,256]{3,2,1,0:T(4,128)S(1)} %bitcast.133, bf16[1,2,128,64,256]{4,3,2,1,0:T(8,128)(2,1)S(1)} %copy-done.1), custom_call_target="tpu_custom_call" | custom-call | flops 1073741824 | bytes 9437184 | tf_op jit(solution)/shard_map/chunk_attention/pallas_call | solution.py:227
  66.8 1.1 reshape_reshape.16
  67.9 4.2 %all-to-all-start.1 = ((bf16[8,2,5120]{2,1,0:T(2,128)(2,1)}), bf16[8,2,5120]{2,1,0:T(2,128)(2,1)}, u32[]{:S(2)}, u32[]{:S(2)}) async-start(bf16[8,2,5120]{2,1,0:T(2,128)(2,1)} %reshape.263), calls=%async_computation.1 | async-start | bytes 327680 | tf_op jit(solution)/shard_map/all_to_all | solution.py:166
  72.0 14.8 %convolution_convert_fusion.3 = bf16[64,8192]{1,0:T(8,128)(2,1)} fusion(bf16[64,2048]{1,0:T(8,128)(2,1)S(1)} %reshape_reshape.16, bf16[2048,8192]{1,0:T(8,128)(2,1)} %param.15), kind=kOutput, calls=%fused_computation.5 | convolution fusion | flops 2148007936 | bytes 34865152 | tf_op jit(solution)/shard_map/dot_general | solution.py:252
  87.2 1.0 reshape.264
  89.8 3.4 %copy-done.2 = bf16[1,2,128,64,256]{4,3,2,1,0:T(8,128)(2,1)S(1)} copy-done((bf16[1,2,128,64,256]{4,3,2,1,0:T(8,128)(2,1)S(1)}, bf16[1,2,128,64,256]{4,3,2,1,0:T(8,128)(2,1)}, u32[]{:S(2)}) %copy-start.2) | copy-done | bytes 8388632
  93.2 5.5 %slot_attention.1 = (bf16[16,32,128]{2,1,0:T(8,128)(2,1)S(1)}, bf16[16,4,2,64,256]{4,3,2,1,0:T(8,128)(2,1)S(1)}) custom-call(s32[16,16]{1,0:T(8,128)S(1)} %bitcast.146, s32[16]{0:T(128)S(1)} %slice_reduce_fusion.lengths, s32[16,4]{1,0:T(8,128)S(1)} %slice.108.wanted, bf16[1,16,32,256]{3,2,1,0:T(8,128)(2,1)S(1)} %broadcast_select_fusion.queries, ...), custom_call_target="tpu_custom_call" | custom-call | flops 536870912 | bytes 12582912 | tf_op jit(solution)/shard_map/slot_attention/pallas_call | solution.py:179
  98.7 1.9 copy-done.5
  101.4 4.2 %all-to-all-start.2 = ((bf16[8,2,4096]{2,1,0:T(2,128)(2,1)}), bf16[8,2,4096]{2,1,0:T(2,128)(2,1)}, u32[]{:S(2)}, u32[]{:S(2)}) async-start(bf16[8,2,4096]{2,1,0:T(2,128)(2,1)} %reshape_reshape.15), calls=%async_computation.2 | async-start | bytes 262144 | tf_op jit(solution)/shard_map/all_to_all | solution.py:202
  105.6 3.4 %copy-done.3 = bf16[1,2,128,64,256]{4,3,2,1,0:T(8,128)(2,1)S(1)} copy-done((bf16[1,2,128,64,256]{4,3,2,1,0:T(8,128)(2,1)S(1)}, bf16[1,2,128,64,256]{4,3,2,1,0:T(8,128)(2,1)}, u32[]{:S(2)}) %copy-start.3) | copy-done | bytes 8388632
  108.9 8.5 %chunk_attention.6 = bf16[32,32,128]{2,1,0:T(8,128)(2,1)S(1)} custom-call(s32[32,16]{1,0:T(8,128)S(1)} %get-tuple-element.31.table, s32[32]{0:T(128)S(1)} %squeeze.42.lengths, bf16[4,32,32,256]{3,2,1,0:T(8,128)(2,1)S(1)} %bitcast.130, f32[4,32,4,256]{3,2,1,0:T(4,128)S(1)} %bitcast.134, bf16[1,2,128,64,256]{4,3,2,1,0:T(8,128)(2,1)S(1)} %copy-done.3), custom_call_target="tpu_custom_call" | custom-call | flops 1073741824 | bytes 9437184 | tf_op jit(solution)/shard_map/chunk_attention/pallas_call | solution.py:227
  118.3 1.1 reshape.260
  119.4 3.4 %copy-done.4 = bf16[1,2,128,64,256]{4,3,2,1,0:T(8,128)(2,1)S(1)} copy-done((bf16[1,2,128,64,256]{4,3,2,1,0:T(8,128)(2,1)S(1)}, bf16[1,2,128,64,256]{4,3,2,1,0:T(8,128)(2,1)}, u32[]{:S(2)}) %copy-start.4) | copy-done | bytes 8388632
  122.7 7.4 %chunk_attention.7 = bf16[32,32,128]{2,1,0:T(8,128)(2,1)S(1)} custom-call(s32[32,16]{1,0:T(8,128)S(1)} %get-tuple-element.30.table, s32[32]{0:T(128)S(1)} %squeeze.48.lengths, bf16[4,32,32,256]{3,2,1,0:T(8,128)(2,1)S(1)} %bitcast.131, f32[4,32,4,256]{3,2,1,0:T(4,128)S(1)} %bitcast.135, bf16[1,2,128,64,256]{4,3,2,1,0:T(8,128)(2,1)S(1)} %copy-done.4), custom_call_target="tpu_custom_call" | custom-call | flops 1073741824 | bytes 9437184 | tf_op jit(solution)/shard_map/chunk_attention/pallas_call | solution.py:227
  130.4 4.6 %all-to-all-start.3 = ((bf16[8,2,4,2,64,256]{5,4,3,2,1,0:T(8,128)(2,1)}), bf16[8,2,4,2,64,256]{5,4,3,2,1,0:T(8,128)(2,1)}, u32[]{:S(2)}, u32[]{:S(2)}) async-start(bf16[8,2,4,2,64,256]{5,4,3,2,1,0:T(8,128)(2,1)} %bitcast.136), calls=%async_computation.7 | async-start | bytes 8388608 | tf_op jit(solution)/shard_map/all_to_all | solution.py:198
  135.0 1.0 reshape.268
  137.0 14.8 %convolution_convert_fusion.1 = bf16[64,8192]{1,0:T(8,128)(2,1)} fusion(bf16[64,2048]{1,0:T(8,128)(2,1)S(1)} %reshape.272, bf16[2048,8192]{1,0:T(8,128)(2,1)} %param.15), kind=kOutput, calls=%fused_computation.3 | convolution fusion | flops 2148007936 | bytes 34865152 | tf_op jit(solution)/shard_map/dot_general | solution.py:252
  151.8 15.7 %reduce-scatter.7.cloned.1.call-done = bf16[16,8192]{1,0:T(8,128)(2,1)} async-done(((bf16[64,8192]{1,0:T(8,128)(2,1)}), bf16[16,8192]{1,0:T(8,128)(2,1)}) %reduce-scatter.7.cloned.1.call-update) | async-done | bytes 262160 | tf_op jit(solution)/shard_map/reduce_scatter | solution.py:257
  168.1 14.8 %convolution_convert_fusion = bf16[64,8192]{1,0:T(8,128)(2,1)} fusion(bf16[64,2048]{1,0:T(8,128)(2,1)S(1)} %reshape.273, bf16[2048,8192]{1,0:T(8,128)(2,1)} %param.15), kind=kOutput, calls=%fused_computation.2 | convolution fusion | flops 2148007936 | bytes 34865152 | tf_op jit(solution)/shard_map/dot_general | solution.py:252
  182.9 13.4 %reduce-scatter.9.cloned.1.call-done = bf16[16,8192]{1,0:T(8,128)(2,1)} async-done(((bf16[64,8192]{1,0:T(8,128)(2,1)}), bf16[16,8192]{1,0:T(8,128)(2,1)}) %reduce-scatter.9.cloned.1.call-update) | async-done | bytes 262160 | tf_op jit(solution)/shard_map/reduce_scatter | solution.py:257
  196.9 2.0 copy.82
  199.0 4.9 %gather_fusion = bf16[14,4,2,64,256]{4,3,2,1,0:T(8,128)(2,1)} fusion(bf16[16,4,2,64,256]{4,3,2,1,0:T(8,128)(2,1)} %bitcast.43, s32[1024]{0:T(1024)S(1)} %pad_clamp_fusion), kind=kCustom, calls=%fused_computation | custom fusion | bytes 7340088 | tf_op jit(solution)/shard_map/jit(_take)/gather | solution.py:201
  203.9 21.0 %reduce-scatter.11.cloned.1.call-done = bf16[16,8192]{1,0:T(8,128)(2,1)} async-done(((bf16[64,8192]{1,0:T(8,128)(2,1)}), bf16[16,8192]{1,0:T(8,128)(2,1)}) %reduce-scatter.11.cloned.1.call-update) | async-done | bytes 262160 | tf_op jit(solution)/shard_map/reduce_scatter | solution.py:257
  224.9 1.0 pad_maximum_fusion.1
  226.0 1.5 broadcast_in_dim_reshape.4
  (109 shorter events, 16.6 us)
Async XLA Ops:
  11.2 7.2 %copy-start.10 = (s32[1,128,16]{1,2,0:T(8,128)S(1)}, s32[1,128,16]{1,2,0:T(8,128)}, u32[]{:S(2)}) copy-start(s32[1,128,16]{1,2,0:T(8,128)} %param.11) | copy-start | bytes 24580
  11.2 7.8 %copy-start.12 = (s32[1,128]{1,0:T(1,128)S(1)}, s32[1,128]{1,0:T(1,128)}, u32[]{:S(2)}) copy-start(s32[1,128]{1,0:T(1,128)} %param.12) | copy-start | bytes 1540
  11.2 8.7 %copy-start.6 = (bf16[1,128,2,2,256]{4,3,2,1,0:T(2,128)(2,1)S(1)}, bf16[1,128,2,2,256]{4,3,2,1,0:T(2,128)(2,1)}, u32[]{:S(2)}) copy-start(bf16[1,128,2,2,256]{4,3,2,1,0:T(2,128)(2,1)} %param.9) | copy-start | bytes 786436
  13.2 54.7 %all-to-all-start = ((s32[8,2,21]{2,1,0:T(2,128)}), s32[8,2,21]{2,1,0:T(2,128)S(1)}, u32[]{:S(2)}, u32[]{:S(2)}) async-start(s32[8,2,21]{2,1,0:T(2,128)} %bitcast.28), calls=%async_computation | async-start | bytes 16384 | tf_op jit(solution)/shard_map/all_to_all | solution.py:163
  18.4 117.6 %reduce-scatter.5.cloned.1.call-start = ((), (), s32[]{:S(2)}) async-start(), calls=%async_computation.8 | async-start | bytes 1310720 | tf_op jit(solution)/shard_map/reduce_scatter | solution.py:257
  22.9 3.4 %copy-start = (bf16[1,2,128,64,256]{4,3,2,1,0:T(8,128)(2,1)S(1)}, bf16[1,2,128,64,256]{4,3,2,1,0:T(8,128)(2,1)}, u32[]{:S(2)}) copy-start(bf16[1,2,128,64,256]{4,3,2,1,0:T(8,128)(2,1)} %pool.9) | copy-start | bytes 25165828
  36.1 15.7 %slice-start = ((bf16[1,128,2,2,256]{4,3,2,1,0:T(2,128)(2,1)}), bf16[1,14,2,2,256]{4,3,2,1,0:T(2,128)(2,1)S(1)}, s32[]{:S(2)}) async-start(bf16[1,128,2,2,256]{4,3,2,1,0:T(2,128)(2,1)} %param.9), calls=%async_computation.12 | async-start | bytes 57344 | tf_op jit(solution)/shard_map/slice | solution.py:157
  52.3 3.4 %copy-start.1 = (bf16[1,2,128,64,256]{4,3,2,1,0:T(8,128)(2,1)S(1)}, bf16[1,2,128,64,256]{4,3,2,1,0:T(8,128)(2,1)}, u32[]{:S(2)}) copy-start(bf16[1,2,128,64,256]{4,3,2,1,0:T(8,128)(2,1)} %pool.9) | copy-start | bytes 25165828
  67.9 19.3 %all-to-all-start.1 = ((bf16[8,2,5120]{2,1,0:T(2,128)(2,1)}), bf16[8,2,5120]{2,1,0:T(2,128)(2,1)}, u32[]{:S(2)}, u32[]{:S(2)}) async-start(bf16[8,2,5120]{2,1,0:T(2,128)(2,1)} %reshape.263), calls=%async_computation.1 | async-start | bytes 327680 | tf_op jit(solution)/shard_map/all_to_all | solution.py:166
  89.8 3.4 %copy-start.2 = (bf16[1,2,128,64,256]{4,3,2,1,0:T(8,128)(2,1)S(1)}, bf16[1,2,128,64,256]{4,3,2,1,0:T(8,128)(2,1)}, u32[]{:S(2)}) copy-start(bf16[1,2,128,64,256]{4,3,2,1,0:T(8,128)(2,1)} %pool.9) | copy-start | bytes 25165828
  98.7 1.9 copy-start.5
  101.4 29.0 %all-to-all-start.2 = ((bf16[8,2,4096]{2,1,0:T(2,128)(2,1)}), bf16[8,2,4096]{2,1,0:T(2,128)(2,1)}, u32[]{:S(2)}, u32[]{:S(2)}) async-start(bf16[8,2,4096]{2,1,0:T(2,128)(2,1)} %reshape_reshape.15), calls=%async_computation.2 | async-start | bytes 262144 | tf_op jit(solution)/shard_map/all_to_all | solution.py:202
  105.6 3.4 %copy-start.3 = (bf16[1,2,128,64,256]{4,3,2,1,0:T(8,128)(2,1)S(1)}, bf16[1,2,128,64,256]{4,3,2,1,0:T(8,128)(2,1)}, u32[]{:S(2)}) copy-start(bf16[1,2,128,64,256]{4,3,2,1,0:T(8,128)(2,1)} %pool.9) | copy-start | bytes 25165828
  119.4 3.4 %copy-start.4 = (bf16[1,2,128,64,256]{4,3,2,1,0:T(8,128)(2,1)S(1)}, bf16[1,2,128,64,256]{4,3,2,1,0:T(8,128)(2,1)}, u32[]{:S(2)}) copy-start(bf16[1,2,128,64,256]{4,3,2,1,0:T(8,128)(2,1)} %pool.9) | copy-start | bytes 25165828
  130.4 68.6 %all-to-all-start.3 = ((bf16[8,2,4,2,64,256]{5,4,3,2,1,0:T(8,128)(2,1)}), bf16[8,2,4,2,64,256]{5,4,3,2,1,0:T(8,128)(2,1)}, u32[]{:S(2)}, u32[]{:S(2)}) async-start(bf16[8,2,4,2,64,256]{5,4,3,2,1,0:T(8,128)(2,1)} %bitcast.136), calls=%async_computation.7 | async-start | bytes 8388608 | tf_op jit(solution)/shard_map/all_to_all | solution.py:198
  134.9 32.6 %reduce-scatter.7.cloned.1.call-start = ((), (), s32[]{:S(2)}) async-start(), calls=%async_computation.9 | async-start | bytes 1310720 | tf_op jit(solution)/shard_map/reduce_scatter | solution.py:257
  136.0 60.3 %reduce-scatter.9.cloned.1.call-start = ((), (), s32[]{:S(2)}) async-start(), calls=%async_computation.10 | async-start | bytes 1310720 | tf_op jit(solution)/shard_map/reduce_scatter | solution.py:257
  167.6 57.3 %reduce-scatter.11.cloned.1.call-start = ((), (), s32[]{:S(2)}) async-start(), calls=%async_computation.11 | async-start | bytes 1310720 | tf_op jit(solution)/shard_map/reduce_scatter | solution.py:257
  168.0 28.6 %copy-start.11 = (s32[1,14,1]{1,2,0:T(1,128)S(1)}, s32[1,14,1]{1,2,0:T(1,128)}, u32[]{:S(2)}) copy-start(s32[1,14,1]{1,2,0:T(1,128)} %param.13) | copy-start | bytes 172
  199.0 26.0 %copy-start.7 = (bf16[16,8192]{1,0:T(8,128)(2,1)S(1)}, bf16[16,8192]{1,0:T(8,128)(2,1)}, u32[]{:S(2)}) copy-start(bf16[16,8192]{1,0:T(8,128)(2,1)} %reduce-scatter.5.cloned.1.call-done) | copy-start | bytes 786436
  199.0 26.0 %copy-start.8 = (bf16[16,8192]{1,0:T(8,128)(2,1)S(1)}, bf16[16,8192]{1,0:T(8,128)(2,1)}, u32[]{:S(2)}) copy-start(bf16[16,8192]{1,0:T(8,128)(2,1)} %reduce-scatter.7.cloned.1.call-done) | copy-start | bytes 786436
  199.0 26.0 %copy-start.9 = (bf16[16,8192]{1,0:T(8,128)(2,1)S(1)}, bf16[16,8192]{1,0:T(8,128)(2,1)}, u32[]{:S(2)}) copy-start(bf16[16,8192]{1,0:T(8,128)(2,1)} %reduce-scatter.9.cloned.1.call-done) | copy-start | bytes 786436
Sparse Core Ops, SparseCore 0:
  50.9 28.8 reduce-scatter.4
  138.8 28.7 reduce-scatter.6
  170.4 25.7 reduce-scatter.8
  199.1 25.7 reduce-scatter.10

commit v2 on v1

--- a/solution.py
+++ b/solution.py
@@ -11,7 +11,9 @@
 HEAD_SIZE = 128
 MIGRANTS = 14
 COPIED = 4
-CHUNKS = 4
+CHUNKS = 2
+DIGIT = 128
+TILE = 512
 NEG_FILL = -1e30
 
 
@@ -89,6 +91,35 @@
     lax.fori_loop(0, out.shape[0] // unroll, step, 0)
 
 
+def project_kernel(rows, weight, out):
+    out[...] = jnp.dot(
+        rows[...], weight[...], preferred_element_type=jnp.float32
+    ).astype(out.dtype)
+
+
+def project(rows, weight):
+    count, depth = rows.shape
+    columns = weight.shape[1]
+    tile = math.gcd(columns, TILE)
+    return pl.pallas_call(
+        project_kernel,
+        grid=(columns // tile,),
+        out_shape=jax.ShapeDtypeStruct((count, columns), rows.dtype),
+        in_specs=[
+            pl.BlockSpec((count, depth), lambda i: (0, 0)),
+            pl.BlockSpec((depth, tile), lambda i: (0, i)),
+        ],
+        out_specs=pl.BlockSpec((count, tile), lambda i: (0, i)),
+        compiler_params=pltpu.CompilerParams(vmem_limit_bytes=24 * 2**20),
+        cost_estimate=pl.CostEstimate(
+            flops=2 * count * depth * columns,
+            bytes_accessed=2 * (depth * columns + count * (depth + columns)),
+            transcendentals=0,
+        ),
+        name="project",
+    )(rows, weight)
+
+
 def unroll_of(count):
     return next(u for u in (4, 2, 1) if count % u == 0)
 
@@ -150,26 +181,30 @@
     mig_ints = jnp.concatenate(
         [mig_table, mig_wanted, lengths[0, staying:, None]], axis=1
     )
-    send_ints = jnp.sum(jnp.where(placing[:, :, None], mig_ints[None], 0), axis=1)
+    ints = mig_ints.shape[1]
     mig_rows = jnp.concatenate(
         [
             queries[0, staying:].reshape(MIGRANTS, -1),
             step_key_value[0, staying:].reshape(MIGRANTS, -1),
+            (mig_ints // DIGIT).astype(jnp.bfloat16),
+            (mig_ints % DIGIT).astype(jnp.bfloat16),
+            jnp.zeros((MIGRANTS, -2 * ints % 128), jnp.bfloat16),
         ],
         axis=1,
     )
     place = placing.astype(jnp.bfloat16)
     send_rows = jnp.dot(place, mig_rows, preferred_element_type=jnp.float32).astype(jnp.bfloat16)
-    got_ints = lax.all_to_all(
-        send_ints.reshape(replicas, capacity, -1), "replica", 0, 0, tiled=True
-    ).reshape(slots, -1)
     got_rows = lax.all_to_all(
         send_rows.reshape(replicas, capacity, -1), "replica", 0, 0, tiled=True
     ).reshape(slots, -1)
 
+    tail = 2 * width + 4 * kv_width
+    digits = got_rows[:, tail : tail + 2 * ints].astype(jnp.int32)
+    got_ints = digits[:, :ints] * DIGIT + digits[:, ints:]
+
     smem = pl.BlockSpec(memory_space=pltpu.SMEM)
     vmem = pl.BlockSpec(memory_space=pltpu.VMEM)
-    params = pltpu.CompilerParams(vmem_limit_bytes=40 * 2**20)
+    params = pltpu.CompilerParams(vmem_limit_bytes=28 * 2**20)
 
     slot_cost = pl.CostEstimate(
         flops=4 * slots * height * pages * page_len * kv_width,
@@ -192,7 +227,7 @@
         got_ints[:, pages + COPIED],
         got_ints[:, pages : pages + COPIED],
         spread(got_rows[:, : 2 * width].reshape(slots, 2, width))[None],
-        got_rows[:, 2 * width :].astype(jnp.float32).reshape(1, slots, 4, kv_width),
+        got_rows[:, 2 * width : tail].astype(jnp.float32).reshape(1, slots, 4, kv_width),
         replica_page_store,
     )
     incoming = lax.all_to_all(
@@ -249,9 +284,7 @@
                 piece = mig_att[first - staying : low + share - staying]
                 att = lax.dynamic_update_slice(att, piece, (at, 0, 0))
         attention.append(att)
-        product = jnp.dot(
-            att.reshape(chunk_rows * 2, width), out_weight, preferred_element_type=jnp.float32
-        ).astype(jnp.bfloat16)
+        product = project(att.reshape(chunk_rows * 2, width), out_weight)
         if projected:
             product, projected[-1] = lax.optimization_barrier((product, projected[-1]))
         projected.append(lax.psum_scatter(product, "tensor", scatter_dimension=0, tiled=True))

time: 235 us -> 198 us (0.84)
  matrix products: 59.6 us -> 0.41 us
  Pallas kernels: 40.7 us -> 76.9 us
  local copies, waits for them, and re-layouts: 46 us -> 33.7 us
  starting transfers between devices: 18.2 us -> 13.3 us
    dot_general x4 -> x0, matrix products: 59.1 us -> none  [body(): jnp.dot(att.reshape(chunk_rows * 2, width), out_weight, preferred_element...]
    reduce_scatter x4 -> x2, waiting for transfers between devices: 50.1 us -> 0.01 us  [body(): lax.psum_scatter(product, 'tensor', scatter_dimension=0, tiled=True)]
    all_to_all x1, waiting for transfers between devices: 0.01 us -> 46.5 us  [body(): lax.all_to_all(sending.reshape((replicas, capacity) + sending.shape[1:]),...]
    pallas_call x0 -> x2, Pallas kernels: none -> 37.4 us  [project(): pl.pallas_call(project_kernel, grid=(columns // tile,), out_shape=jax.Sha...]
    unnamed x34 -> x29, local copies, waits for them, and re-layouts: 22.7 us -> 15.9 us
    all_to_all x1, waiting for transfers between devices: 0.01 us -> 5.84 us  [body(): lax.all_to_all(send_rows.reshape(replicas, capacity, -1), 'replica', 0, 0...]
    all_to_all x1 -> x0, starting transfers between devices: 5.17 us -> none  [body(): lax.all_to_all(send_ints.reshape(replicas, capacity, -1), 'replica', 0, 0...]
    pallas_call x4 -> x2, Pallas kernels: 35.2 us -> 34 us  [body(): pl.pallas_call(functools.partial(chunk_kernel, sizes, unroll, row_of, sta...]
  transfers between devices with their start and end apart: 8 -> 5, of which waited for: 3 -> 2; matrix products, arithmetic and copies ran while one was open for 36% -> 7% of each run, Pallas kernels for 17% -> 20%
where the time goes in v2:
time: 198 us; the launch traced here: 197 us
  Pallas kernels  76.9 us (39%)
  waiting for transfers between devices  52.4 us (26%)
  local copies, waits for them, and re-layouts  33.7 us (17%)
  between operations  14.4 us (7%)
  starting transfers between devices  13.3 us (7%)
  other arithmetic  5.48 us (3%)
    all_to_all x1, waiting for transfers between devices, body(): lax.all_to_all(sending.reshape((replicas, capacity) + sending.shape[1:]),...  46.5 us
    pallas_call x2, Pallas kernels, project(): pl.pallas_call(project_kernel, grid=(columns // tile,), out_shape=jax.Sha...  37.4 us
    pallas_call x2, Pallas kernels, body(): pl.pallas_call(functools.partial(chunk_kernel, sizes, unroll, row_of, sta...  34 us
    unnamed x29, local copies, waits for them, and re-layouts  15.9 us
    all_to_all x1, waiting for transfers between devices, body(): lax.all_to_all(send_rows.reshape(replicas, capacity, -1), 'replica', 0, 0...  5.84 us
    pallas_call x1, Pallas kernels, body(): pl.pallas_call(functools.partial(slot_kernel, sizes, unroll_of(slots)), o...  5.59 us
    all_to_all x1, starting transfers between devices, body(): lax.all_to_all(send_rows.reshape(replicas, capacity, -1), 'replica', 0, 0...  5.18 us
    gather x1, local copies, waits for them, and re-layouts, body(): arrived = jnp.take(incoming, slot_of, axis=0, mode='clip')  4.91 us
  transfers between devices with their start and end apart: 5, of which 2 were waited for; matrix products, arithmetic and copies ran while one was open for 7% of the time, Pallas kernels for 20%

profile of v2, /device:TPU:0, one launch (start us, length us, event | category | flops | bytes accessed | tf_op | source)
XLA Modules:
  0.0 196.7 jit_solution(17062225869130740792)
XLA Ops:
  7.2 0.5 broadcast.232
  7.7 1.3 reduce.13
  9.3 0.8 reshape_squeeze.15
  10.2 1.1 reshape.234
  11.4 1.7 reshape_squeeze.17
  13.4 0.3 broadcast_in_dim.82
  14.0 3.4 %copy-done = bf16[1,2,128,64,256]{4,3,2,1,0:T(8,128)(2,1)S(1)} copy-done((bf16[1,2,128,64,256]{4,3,2,1,0:T(8,128)(2,1)S(1)}, bf16[1,2,128,64,256]{4,3,2,1,0:T(8,128)(2,1)}, u32[]{:S(2)}) %copy-start) | copy-done | bytes 8388632
  17.4 18.6 %chunk_attention.2 = bf16[64,32,128]{2,1,0:T(8,128)(2,1)S(1)} custom-call(s32[64,16]{1,0:T(8,128)S(1)} %bitcast.90, s32[64]{0:T(128)S(1)} %squeeze.26.lengths, bf16[2,64,32,256]{3,2,1,0:T(8,128)(2,1)S(1)} %bitcast.82, f32[2,64,4,256]{3,2,1,0:T(4,128)S(1)} %bitcast.84, bf16[1,2,128,64,256]{4,3,2,1,0:T(8,128)(2,1)S(1)} %copy-done), custom_call_target="tpu_custom_call" | custom-call | flops 2147483648 | bytes 9437184 | tf_op jit(solution)/shard_map/chunk_attention/pallas_call | solution.py:262
  36.0 0.9 copy.101
  36.9 1.3 reshape_reshape.13.rows
  38.2 18.2 %project.3 = bf16[128,8192]{1,0:T(8,128)(2,1)S(1)} custom-call(bf16[128,2048]{1,0:T(8,128)(2,1)S(1)} %reshape_reshape.13.rows, bf16[2048,8192]{1,0:T(8,128)(2,1)} %weight.3), custom_call_target="tpu_custom_call" | custom-call | flops 4294967296 | bytes 36175872 | tf_op jit(solution)/shard_map/project/pallas_call | solution.py:104
  56.4 1.3 copy-done.3
  57.7 0.7 copy-done.8
  59.1 1.0 gather_fusion.1
  60.2 1.0 slice_bitcast_fusion.1
  61.9 0.7 reshape.217
  62.7 5.2 %all-to-all-start = ((bf16[8,2,5248]{2,1,0:T(2,128)(2,1)}), bf16[8,2,5248]{2,1,0:T(2,128)(2,1)S(1)}, u32[]{:S(2)}, u32[]{:S(2)}) async-start(bf16[8,2,5248]{2,1,0:T(2,128)(2,1)} %reshape.217), calls=%async_computation | async-start | bytes 335872 | tf_op jit(solution)/shard_map/all_to_all | solution.py:197
  67.9 5.8 %all-to-all-done = bf16[8,2,5248]{2,1,0:T(2,128)(2,1)S(1)} async-done(((bf16[8,2,5248]{2,1,0:T(2,128)(2,1)}), bf16[8,2,5248]{2,1,0:T(2,128)(2,1)S(1)}, u32[]{:S(2)}, u32[]{:S(2)}) %all-to-all-start) | async-done | bytes 167968 | tf_op jit(solution)/shard_map/all_to_all | solution.py:197
  74.4 3.4 %copy-done.1 = bf16[1,2,128,64,256]{4,3,2,1,0:T(8,128)(2,1)S(1)} copy-done((bf16[1,2,128,64,256]{4,3,2,1,0:T(8,128)(2,1)S(1)}, bf16[1,2,128,64,256]{4,3,2,1,0:T(8,128)(2,1)}, u32[]{:S(2)}) %copy-start.1) | copy-done | bytes 8388632
  77.8 5.6 %slot_attention.1 = (bf16[16,32,128]{2,1,0:T(8,128)(2,1)S(1)}, bf16[16,4,2,64,256]{4,3,2,1,0:T(8,128)(2,1)S(1)}) custom-call(s32[16,16]{1,0:T(8,128)S(1)} %bitcast.92, s32[16]{0:T(128)S(1)} %slice_reduce_fusion.lengths, s32[16,4]{1,0:T(8,128)S(1)} %slice.85.wanted, bf16[1,16,32,256]{3,2,1,0:T(8,128)(2,1)S(1)} %broadcast_select_fusion.queries, ...), custom_call_target="tpu_custom_call" | custom-call | flops 536870912 | bytes 12582912 | tf_op jit(solution)/shard_map/slot_attention/pallas_call | solution.py:214
  83.4 1.9 copy-done.4
  85.4 0.7 reshape_reshape.12
  86.1 3.4 %all-to-all-start.1 = ((bf16[8,2,4096]{2,1,0:T(2,128)(2,1)}), bf16[8,2,4096]{2,1,0:T(2,128)(2,1)S(1)}, u32[]{:S(2)}, u32[]{:S(2)}) async-start(bf16[8,2,4096]{2,1,0:T(2,128)(2,1)} %reshape_reshape.12), calls=%async_computation.1 | async-start | bytes 262144 | tf_op jit(solution)/shard_map/all_to_all | solution.py:237
  89.5 3.4 %copy-done.2 = bf16[1,2,128,64,256]{4,3,2,1,0:T(8,128)(2,1)S(1)} copy-done((bf16[1,2,128,64,256]{4,3,2,1,0:T(8,128)(2,1)S(1)}, bf16[1,2,128,64,256]{4,3,2,1,0:T(8,128)(2,1)}, u32[]{:S(2)}) %copy-start.2) | copy-done | bytes 8388632
  93.0 15.4 %chunk_attention.3 = bf16[64,32,128]{2,1,0:T(8,128)(2,1)S(1)} custom-call(s32[64,16]{1,0:T(8,128)S(1)} %bitcast.89, s32[64]{0:T(128)S(1)} %squeeze.28.lengths, bf16[2,64,32,256]{3,2,1,0:T(8,128)(2,1)S(1)} %bitcast.83, f32[2,64,4,256]{3,2,1,0:T(4,128)S(1)} %bitcast.85, bf16[1,2,128,64,256]{4,3,2,1,0:T(8,128)(2,1)S(1)} %copy-done.2), custom_call_target="tpu_custom_call" | custom-call | flops 2147483648 | bytes 9437184 | tf_op jit(solution)/shard_map/chunk_attention/pallas_call | solution.py:262
  109.3 19.1 %project.2 = bf16[128,8192]{1,0:T(8,128)(2,1)} custom-call(bf16[128,2048]{1,0:T(8,128)(2,1)S(1)} %reshape.225.rows, bf16[2048,8192]{1,0:T(8,128)(2,1)} %weight.3), custom_call_target="tpu_custom_call" | custom-call | flops 4294967296 | bytes 36175872 | tf_op jit(solution)/shard_map/project/pallas_call | solution.py:104
  128.4 4.7 %all-to-all-start.2 = ((bf16[8,2,4,2,64,256]{5,4,3,2,1,0:T(8,128)(2,1)}), bf16[8,2,4,2,64,256]{5,4,3,2,1,0:T(8,128)(2,1)}, u32[]{:S(2)}, u32[]{:S(2)}) async-start(bf16[8,2,4,2,64,256]{5,4,3,2,1,0:T(8,128)(2,1)} %bitcast.86), calls=%async_computation.4 | async-start | bytes 8388608 | tf_op jit(solution)/shard_map/all_to_all | solution.py:233
  133.3 2.5 %pad_maximum_fusion = bf16[4,2,16,2,2048]{4,3,2,1,0:T(2,128)(2,1)} fusion(bf16[4,1,16,2,2048]{4,3,2,1,0:T(2,128)(2,1)S(1)} %bitcast.98, bf16[4,1,16,2,2048]{4,3,2,1,0:T(2,128)(2,1)S(1)} %bitcast.101), kind=kLoop, calls=%fused_computation.5 | loop fusion | flops 524288 | bytes 2097152 | tf_op jit(solution)/shard_map/stack | solution.py:291
  135.8 46.5 %all-to-all-done.2 = bf16[8,2,4,2,64,256]{5,4,3,2,1,0:T(8,128)(2,1)} async-done(((bf16[8,2,4,2,64,256]{5,4,3,2,1,0:T(8,128)(2,1)}), bf16[8,2,4,2,64,256]{5,4,3,2,1,0:T(8,128)(2,1)}, u32[]{:S(2)}, u32[]{:S(2)}) %all-to-all-start.2) | async-done | bytes 4194336 | tf_op jit(solution)/shard_map/all_to_all | solution.py:233
  182.3 4.9 %gather_fusion = bf16[14,4,2,64,256]{4,3,2,1,0:T(8,128)(2,1)} fusion(bf16[16,4,2,64,256]{4,3,2,1,0:T(8,128)(2,1)} %bitcast.30, s32[1024]{0:T(1024)S(1)} %pad_clamp_fusion), kind=kCustom, calls=%fused_computation | custom fusion | bytes 7340088 | tf_op jit(solution)/shard_map/jit(_take)/gather | solution.py:236
  187.2 1.1 pad_maximum_fusion.1
  188.3 1.5 broadcast_in_dim_reshape.4
  (81 shorter events, 4.2 us)
Async XLA Ops:
  7.2 121.2 %reduce-scatter.3.cloned.1.call-start = ((), (), s32[]{:S(2)}) async-start(), calls=%async_computation.5 | async-start | bytes 2621440 | tf_op jit(solution)/shard_map/reduce_scatter | solution.py:290
  14.0 3.4 %copy-start = (bf16[1,2,128,64,256]{4,3,2,1,0:T(8,128)(2,1)S(1)}, bf16[1,2,128,64,256]{4,3,2,1,0:T(8,128)(2,1)}, u32[]{:S(2)}) copy-start(bf16[1,2,128,64,256]{4,3,2,1,0:T(8,128)(2,1)} %pool.5) | copy-start | bytes 25165828
  56.4 1.3 copy-start.3
  57.7 0.7 copy-start.8
  57.7 0.8 copy-start.10
  57.7 0.9 copy-start.7
  59.1 1.0 slice-start
  59.1 2.4 %copy-start.9 = (s32[1,14,1]{1,2,0:T(1,128)S(1)}, s32[1,14,1]{1,2,0:T(1,128)}, u32[]{:S(2)}) copy-start(s32[1,14,1]{1,2,0:T(1,128)} %param.13) | copy-start | bytes 172
  62.7 11.1 %all-to-all-start = ((bf16[8,2,5248]{2,1,0:T(2,128)(2,1)}), bf16[8,2,5248]{2,1,0:T(2,128)(2,1)S(1)}, u32[]{:S(2)}, u32[]{:S(2)}) async-start(bf16[8,2,5248]{2,1,0:T(2,128)(2,1)} %reshape.217), calls=%async_computation | async-start | bytes 335872 | tf_op jit(solution)/shard_map/all_to_all | solution.py:197
  74.4 3.4 %copy-start.1 = (bf16[1,2,128,64,256]{4,3,2,1,0:T(8,128)(2,1)S(1)}, bf16[1,2,128,64,256]{4,3,2,1,0:T(8,128)(2,1)}, u32[]{:S(2)}) copy-start(bf16[1,2,128,64,256]{4,3,2,1,0:T(8,128)(2,1)} %pool.5) | copy-start | bytes 25165828
  83.4 1.9 copy-start.4
  86.1 22.5 %all-to-all-start.1 = ((bf16[8,2,4096]{2,1,0:T(2,128)(2,1)}), bf16[8,2,4096]{2,1,0:T(2,128)(2,1)S(1)}, u32[]{:S(2)}, u32[]{:S(2)}) async-start(bf16[8,2,4096]{2,1,0:T(2,128)(2,1)} %reshape_reshape.12), calls=%async_computation.1 | async-start | bytes 262144 | tf_op jit(solution)/shard_map/all_to_all | solution.py:237
  89.5 97.7 %reduce-scatter.5.cloned.1.call-start = ((), (), s32[]{:S(2)}) async-start(), calls=%async_computation.6 | async-start | bytes 2621440 | tf_op jit(solution)/shard_map/reduce_scatter | solution.py:290
  89.5 3.4 %copy-start.2 = (bf16[1,2,128,64,256]{4,3,2,1,0:T(8,128)(2,1)S(1)}, bf16[1,2,128,64,256]{4,3,2,1,0:T(8,128)(2,1)}, u32[]{:S(2)}) copy-start(bf16[1,2,128,64,256]{4,3,2,1,0:T(8,128)(2,1)} %pool.5) | copy-start | bytes 25165828
  128.4 4.7 %copy-start.5 = (bf16[64,2,2,8,128]{4,3,1,2,0:T(8,128)(2,1)S(1)}, bf16[64,2,2,8,128]{4,3,1,2,0:T(8,128)(2,1)}, u32[]{:S(2)}) copy-start(bf16[64,2,2,8,128]{4,3,1,2,0:T(8,128)(2,1)} %copy.101) | copy-start | bytes 1572868
  128.4 53.8 %all-to-all-start.2 = ((bf16[8,2,4,2,64,256]{5,4,3,2,1,0:T(8,128)(2,1)}), bf16[8,2,4,2,64,256]{5,4,3,2,1,0:T(8,128)(2,1)}, u32[]{:S(2)}, u32[]{:S(2)}) async-start(bf16[8,2,4,2,64,256]{5,4,3,2,1,0:T(8,128)(2,1)} %bitcast.86), calls=%async_computation.4 | async-start | bytes 8388608 | tf_op jit(solution)/shard_map/all_to_all | solution.py:233
  182.3 4.9 %copy-start.6 = (bf16[32,8192]{1,0:T(8,128)(2,1)S(1)}, bf16[32,8192]{1,0:T(8,128)(2,1)}, u32[]{:S(2)}) copy-start(bf16[32,8192]{1,0:T(8,128)(2,1)} %reduce-scatter.3.cloned.1.call-done) | copy-start | bytes 1572868
Sparse Core Ops, SparseCore 0:
  57.9 46.6 reduce-scatter.2
  128.6 45.4 reduce-scatter.4

commit v3 on v1

--- a/solution.py
+++ b/solution.py
@@ -11,7 +11,8 @@
 HEAD_SIZE = 128
 MIGRANTS = 14
 COPIED = 4
-CHUNKS = 4
+CHUNKS = 2
+DIGIT = 128
 NEG_FILL = -1e30
 
 
@@ -150,26 +151,30 @@
     mig_ints = jnp.concatenate(
         [mig_table, mig_wanted, lengths[0, staying:, None]], axis=1
     )
-    send_ints = jnp.sum(jnp.where(placing[:, :, None], mig_ints[None], 0), axis=1)
+    ints = mig_ints.shape[1]
     mig_rows = jnp.concatenate(
         [
             queries[0, staying:].reshape(MIGRANTS, -1),
             step_key_value[0, staying:].reshape(MIGRANTS, -1),
+            (mig_ints // DIGIT).astype(jnp.bfloat16),
+            (mig_ints % DIGIT).astype(jnp.bfloat16),
+            jnp.zeros((MIGRANTS, -2 * ints % 128), jnp.bfloat16),
         ],
         axis=1,
     )
     place = placing.astype(jnp.bfloat16)
     send_rows = jnp.dot(place, mig_rows, preferred_element_type=jnp.float32).astype(jnp.bfloat16)
-    got_ints = lax.all_to_all(
-        send_ints.reshape(replicas, capacity, -1), "replica", 0, 0, tiled=True
-    ).reshape(slots, -1)
     got_rows = lax.all_to_all(
         send_rows.reshape(replicas, capacity, -1), "replica", 0, 0, tiled=True
     ).reshape(slots, -1)
 
+    tail = 2 * width + 4 * kv_width
+    digits = got_rows[:, tail : tail + 2 * ints].astype(jnp.int32)
+    got_ints = digits[:, :ints] * DIGIT + digits[:, ints:]
+
     smem = pl.BlockSpec(memory_space=pltpu.SMEM)
     vmem = pl.BlockSpec(memory_space=pltpu.VMEM)
-    params = pltpu.CompilerParams(vmem_limit_bytes=40 * 2**20)
+    params = pltpu.CompilerParams(vmem_limit_bytes=28 * 2**20)
 
     slot_cost = pl.CostEstimate(
         flops=4 * slots * height * pages * page_len * kv_width,
@@ -192,13 +197,14 @@
         got_ints[:, pages + COPIED],
         got_ints[:, pages : pages + COPIED],
         spread(got_rows[:, : 2 * width].reshape(slots, 2, width))[None],
-        got_rows[:, 2 * width :].astype(jnp.float32).reshape(1, slots, 4, kv_width),
+        got_rows[:, 2 * width : tail].astype(jnp.float32).reshape(1, slots, 4, kv_width),
         replica_page_store,
     )
+    slot_att, sending, moved_table = lax.optimization_barrier((slot_att, sending, page_table[0]))
+    all_table = by_chunk(moved_table)
     incoming = lax.all_to_all(
         sending.reshape((replicas, capacity) + sending.shape[1:]), "replica", 0, 0, tiled=True
     ).reshape(sending.shape)
-    arrived = jnp.take(incoming, slot_of, axis=0, mode="clip")
     back = lax.all_to_all(
         gathered(slot_att).reshape(replicas, capacity, -1), "replica", 0, 0, tiled=True
     ).reshape(slots, -1)
@@ -210,7 +216,6 @@
 
     all_queries = by_chunk(spread(queries[0]))
     all_fresh = by_chunk(step_key_value[0].astype(jnp.float32).reshape(row_count, 4, kv_width))
-    all_table = by_chunk(page_table[0])
     all_lengths = by_chunk(lengths[0])
     chunk_cost = pl.CostEstimate(
         flops=4 * chunk_rows * height * pages * page_len * kv_width,
@@ -249,12 +254,15 @@
                 piece = mig_att[first - staying : low + share - staying]
                 att = lax.dynamic_update_slice(att, piece, (at, 0, 0))
         attention.append(att)
+        if c == CHUNKS - 1:
+            att, incoming = lax.optimization_barrier((att, incoming))
         product = jnp.dot(
             att.reshape(chunk_rows * 2, width), out_weight, preferred_element_type=jnp.float32
         ).astype(jnp.bfloat16)
         if projected:
             product, projected[-1] = lax.optimization_barrier((product, projected[-1]))
         projected.append(lax.psum_scatter(product, "tensor", scatter_dimension=0, tiled=True))
+    arrived = jnp.take(incoming, slot_of, axis=0, mode="clip")
     attention = jnp.stack([a.reshape(shards, share, 2, width) for a in attention], axis=1)
     attention = attention.reshape(1, row_count, 2, width)
     projected = jnp.concatenate(projected, axis=0).reshape(per_shard, 2, -1)

time: 235 us -> 192 us (0.82)
  matrix products: 59.6 us -> 33.5 us
  local copies, waits for them, and re-layouts: 46 us -> 37.8 us
  starting transfers between devices: 18.2 us -> 14.2 us
    dot_general x4 -> x2, matrix products: 59.1 us -> 33.1 us  [body(): jnp.dot(att.reshape(chunk_rows * 2, width), out_weight, preferred_element...]
    reduce_scatter x4 -> x2, waiting for transfers between devices: 50.1 us -> 35.9 us  [body(): lax.psum_scatter(product, 'tensor', scatter_dimension=0, tiled=True)]
    all_to_all x1, waiting for transfers between devices: 0.01 us -> 12.1 us  [body(): lax.all_to_all(sending.reshape((replicas, capacity) + sending.shape[1:]),...]
    unnamed x34 -> x28, local copies, waits for them, and re-layouts: 22.7 us -> 15.9 us
    all_to_all x1 -> x0, starting transfers between devices: 5.17 us -> none  [body(): lax.all_to_all(send_ints.reshape(replicas, capacity, -1), 'replica', 0, 0...]
    pallas_call x4 -> x2, Pallas kernels: 35.2 us -> 34 us  [body(): pl.pallas_call(functools.partial(chunk_kernel, sizes, unroll, row_of, sta...]
  transfers between devices with their start and end apart: 8 -> 5, of which waited for: 3 -> 2; matrix products, arithmetic and copies ran while one was open for 36% -> 27% of each run, Pallas kernels for 17% -> 18%
where the time goes in v3:
time: 192 us; the launch traced here: 191 us
  waiting for transfers between devices  48.1 us (25%)
  Pallas kernels  39.5 us (21%)
  local copies, waits for them, and re-layouts  37.8 us (20%)
  matrix products  33.5 us (17%)
  between operations  14.4 us (8%)
  starting transfers between devices  14.2 us (7%)
  other arithmetic  3.78 us (2%)
    reduce_scatter x2, waiting for transfers between devices, body(): lax.psum_scatter(product, 'tensor', scatter_dimension=0, tiled=True)  35.9 us
    pallas_call x2, Pallas kernels, body(): pl.pallas_call(functools.partial(chunk_kernel, sizes, unroll, row_of, sta...  34 us
    dot_general x2, matrix products, body(): jnp.dot(att.reshape(chunk_rows * 2, width), out_weight, preferred_element...  33.1 us
    unnamed x28, local copies, waits for them, and re-layouts  15.9 us
    all_to_all x1, waiting for transfers between devices, body(): lax.all_to_all(sending.reshape((replicas, capacity) + sending.shape[1:]),...  12.1 us
    pallas_call x1, Pallas kernels, body(): pl.pallas_call(functools.partial(slot_kernel, sizes, unroll_of(slots)), o...  5.56 us
    all_to_all x1, starting transfers between devices, body(): lax.all_to_all(send_rows.reshape(replicas, capacity, -1), 'replica', 0, 0...  5.17 us
    gather x1, local copies, waits for them, and re-layouts, body(): arrived = jnp.take(incoming, slot_of, axis=0, mode='clip')  4.91 us
  transfers between devices with their start and end apart: 5, of which 2 were waited for; matrix products, arithmetic and copies ran while one was open for 27% of the time, Pallas kernels for 18%

profile of v3, /device:TPU:0, one launch (start us, length us, event | category | flops | bytes accessed | tf_op | source)
XLA Modules:
  0.0 191.2 jit_solution(3080029995149916610)
XLA Ops:
  7.2 1.0 slice_bitcast_fusion.1
  8.3 0.8 slice.56
  9.1 0.7 slice_bitcast_fusion.2
  9.9 0.8 slice.57
  10.8 0.8 copy.98
  11.8 1.0 gather_fusion.1
  13.5 0.7 reshape.214
  14.3 5.2 %all-to-all-start = ((bf16[8,2,5248]{2,1,0:T(2,128)(2,1)}), bf16[8,2,5248]{2,1,0:T(2,128)(2,1)S(1)}, u32[]{:S(2)}, u32[]{:S(2)}) async-start(bf16[8,2,5248]{2,1,0:T(2,128)(2,1)} %reshape.214), calls=%async_computation | async-start | bytes 335872 | tf_op jit(solution)/shard_map/all_to_all | solution.py:167
  19.5 0.7 reshape_squeeze.15
  20.8 1.5 select_bitcast_fusion
  22.9 0.7 reduce.13
  23.7 1.9 copy.108
  26.3 3.4 %copy-done = bf16[1,2,128,64,256]{4,3,2,1,0:T(8,128)(2,1)S(1)} copy-done((bf16[1,2,128,64,256]{4,3,2,1,0:T(8,128)(2,1)S(1)}, bf16[1,2,128,64,256]{4,3,2,1,0:T(8,128)(2,1)}, u32[]{:S(2)}) %copy-start) | copy-done | bytes 8388632
  29.7 5.6 %slot_attention.1 = (bf16[16,32,128]{2,1,0:T(8,128)(2,1)S(1)}, bf16[16,4,2,64,256]{4,3,2,1,0:T(8,128)(2,1)S(1)}) custom-call(s32[16,16]{1,0:T(8,128)S(1)} %bitcast.102, s32[16]{0:T(128)S(1)} %slice_reduce_fusion.lengths, s32[16,4]{1,0:T(8,128)S(1)} %slice.81.wanted, bf16[1,16,32,256]{3,2,1,0:T(8,128)(2,1)S(1)} %broadcast_select_fusion.queries, ...), custom_call_target="tpu_custom_call" | custom-call | flops 536870912 | bytes 12582912 | tf_op jit(solution)/shard_map/slot_attention/pallas_call | solution.py:184
  35.3 2.0 %copy-done.3 = bf16[16,4,2,64,256]{4,3,2,1,0:T(8,128)(2,1)} copy-done((bf16[16,4,2,64,256]{4,3,2,1,0:T(8,128)(2,1)}, bf16[16,4,2,64,256]{4,3,2,1,0:T(8,128)(2,1)S(1)}, u32[]{:S(2)}) %copy-start.3) | copy-done | bytes 4194328
  37.5 0.7 reshape_reshape.12
  38.2 4.2 %all-to-all-start.1 = ((bf16[8,2,4096]{2,1,0:T(2,128)(2,1)}), bf16[8,2,4096]{2,1,0:T(2,128)(2,1)S(1)}, u32[]{:S(2)}, u32[]{:S(2)}) async-start(bf16[8,2,4096]{2,1,0:T(2,128)(2,1)} %reshape_reshape.12), calls=%async_computation.1 | async-start | bytes 262144 | tf_op jit(solution)/shard_map/all_to_all | solution.py:208
  42.4 3.4 %copy-done.1 = bf16[1,2,128,64,256]{4,3,2,1,0:T(8,128)(2,1)S(1)} copy-done((bf16[1,2,128,64,256]{4,3,2,1,0:T(8,128)(2,1)S(1)}, bf16[1,2,128,64,256]{4,3,2,1,0:T(8,128)(2,1)}, u32[]{:S(2)}) %copy-start.1) | copy-done | bytes 8388632
  45.8 18.6 %chunk_attention.2 = bf16[64,32,128]{2,1,0:T(8,128)(2,1)S(1)} custom-call(s32[64,16]{1,0:T(8,128)S(1)} %bitcast.100, s32[64]{0:T(128)S(1)} %squeeze.34.lengths, bf16[2,64,32,256]{3,2,1,0:T(8,128)(2,1)S(1)} %bitcast.91, f32[2,64,4,256]{3,2,1,0:T(4,128)S(1)} %bitcast.93, bf16[1,2,128,64,256]{4,3,2,1,0:T(8,128)(2,1)S(1)} %copy-done.1), custom_call_target="tpu_custom_call" | custom-call | flops 2147483648 | bytes 9437184 | tf_op jit(solution)/shard_map/chunk_attention/pallas_call | solution.py:232
  64.4 0.9 copy.128
  65.3 2.1 %reshape_reshape.13 = bf16[128,2048]{1,0:T(8,128)(2,1)} reshape(bf16[64,2,2,8,128]{4,3,2,1,0:T(8,128)(2,1)} %bitcast.111) | data formatting | bytes 1048576 | tf_op jit(solution)/shard_map/reshape;reshape | solution.py:260
  67.3 4.5 %all-to-all-start.2 = ((bf16[8,2,4,2,64,256]{5,4,3,2,1,0:T(8,128)(2,1)}), bf16[8,2,4,2,64,256]{5,4,3,2,1,0:T(8,128)(2,1)}, u32[]{:S(2)}, u32[]{:S(2)}) async-start(bf16[8,2,4,2,64,256]{5,4,3,2,1,0:T(8,128)(2,1)} %bitcast.97), calls=%async_computation.2 | async-start | bytes 8388608 | tf_op jit(solution)/shard_map/all_to_all | solution.py:205
  71.9 16.6 %convolution_convert_fusion = bf16[128,8192]{1,0:T(8,128)(2,1)} fusion(bf16[128,2048]{1,0:T(8,128)(2,1)} %reshape_reshape.13, bf16[2048,8192]{1,0:T(8,128)(2,1)} %param.15), kind=kOutput, calls=%fused_computation.2 | convolution fusion | flops 4296015872 | bytes 36175872 | tf_op jit(solution)/shard_map/dot_general | solution.py:259
  88.9 3.4 %copy-done.2 = bf16[1,2,128,64,256]{4,3,2,1,0:T(8,128)(2,1)S(1)} copy-done((bf16[1,2,128,64,256]{4,3,2,1,0:T(8,128)(2,1)S(1)}, bf16[1,2,128,64,256]{4,3,2,1,0:T(8,128)(2,1)}, u32[]{:S(2)}) %copy-start.2) | copy-done | bytes 8388632
  92.2 15.4 %chunk_attention.3 = bf16[64,32,128]{2,1,0:T(8,128)(2,1)S(1)} custom-call(s32[64,16]{1,0:T(8,128)S(1)} %bitcast.99, s32[64]{0:T(128)S(1)} %squeeze.36.lengths, bf16[2,64,32,256]{3,2,1,0:T(8,128)(2,1)S(1)} %bitcast.92, f32[2,64,4,256]{3,2,1,0:T(4,128)S(1)} %bitcast.94, bf16[1,2,128,64,256]{4,3,2,1,0:T(8,128)(2,1)S(1)} %copy-done.2), custom_call_target="tpu_custom_call" | custom-call | flops 2147483648 | bytes 9437184 | tf_op jit(solution)/shard_map/chunk_attention/pallas_call | solution.py:232
  108.9 12.1 %all-to-all-done.2 = bf16[8,2,4,2,64,256]{5,4,3,2,1,0:T(8,128)(2,1)} async-done(((bf16[8,2,4,2,64,256]{5,4,3,2,1,0:T(8,128)(2,1)}), bf16[8,2,4,2,64,256]{5,4,3,2,1,0:T(8,128)(2,1)}, u32[]{:S(2)}, u32[]{:S(2)}) %all-to-all-start.2) | async-done | bytes 4194336 | tf_op jit(solution)/shard_map/all_to_all | solution.py:205
  121.8 16.5 %convolution_convert_fusion.1 = bf16[128,8192]{1,0:T(8,128)(2,1)} fusion(bf16[128,2048]{1,0:T(8,128)(2,1)S(1)} %reshape.231, bf16[2048,8192]{1,0:T(8,128)(2,1)} %param.15), kind=kOutput, calls=%fused_computation.3 | convolution fusion | flops 4296015872 | bytes 36175872 | tf_op jit(solution)/shard_map/dot_general | solution.py:259
  138.9 2.0 %copy.117 = bf16[1,128,2,2048]{3,2,1,0:T(2,128)(2,1)} copy(bf16[1,128,2,2048]{3,1,2,0:T(8,128)(2,1)S(1)} %bitcast.108) | data formatting | bytes 2097152
  140.9 4.9 %gather_fusion = bf16[14,4,2,64,256]{4,3,2,1,0:T(8,128)(2,1)} fusion(bf16[16,4,2,64,256]{4,3,2,1,0:T(8,128)(2,1)} %bitcast.30, s32[1024]{0:T(1024)S(1)} %pad_clamp_fusion), kind=kCustom, calls=%fused_computation | custom fusion | bytes 7340088 | tf_op jit(solution)/shard_map/jit(_take)/gather | solution.py:265
  145.8 35.9 %reduce-scatter.5.cloned.1.call-done = bf16[32,8192]{1,0:T(8,128)(2,1)} async-done(((bf16[128,8192]{1,0:T(8,128)(2,1)}), bf16[32,8192]{1,0:T(8,128)(2,1)}) %reduce-scatter.5.cloned.1.call-update) | async-done | bytes 524304 | tf_op jit(solution)/shard_map/reduce_scatter | solution.py:264
  181.8 1.1 pad_maximum_fusion.1
  182.9 1.5 broadcast_in_dim_reshape.4
  (83 shorter events, 6.5 us)
Async XLA Ops:
  11.8 1.2 copy-start.8
  11.8 7.7 %copy-start.4 = (bf16[1,128,2,2048]{3,2,1,0:T(2,128)(2,1)S(1)}, bf16[1,128,2,2048]{3,2,1,0:T(2,128)(2,1)}, u32[]{:S(2)}) copy-start(bf16[1,128,2,2048]{3,2,1,0:T(2,128)(2,1)} %param.8) | copy-start | bytes 3145732
  14.3 11.4 %all-to-all-start = ((bf16[8,2,5248]{2,1,0:T(2,128)(2,1)}), bf16[8,2,5248]{2,1,0:T(2,128)(2,1)S(1)}, u32[]{:S(2)}, u32[]{:S(2)}) async-start(bf16[8,2,5248]{2,1,0:T(2,128)(2,1)} %reshape.214), calls=%async_computation | async-start | bytes 335872 | tf_op jit(solution)/shard_map/all_to_all | solution.py:167
  20.4 1.8 copy-start.6
  20.4 2.5 %copy-start.9 = (s32[1,128]{1,0:T(1,128)S(1)}, s32[1,128]{1,0:T(1,128)}, u32[]{:S(2)}) copy-start(s32[1,128]{1,0:T(1,128)} %param.12) | copy-start | bytes 1540
  26.3 3.4 %copy-start = (bf16[1,2,128,64,256]{4,3,2,1,0:T(8,128)(2,1)S(1)}, bf16[1,2,128,64,256]{4,3,2,1,0:T(8,128)(2,1)}, u32[]{:S(2)}) copy-start(bf16[1,2,128,64,256]{4,3,2,1,0:T(8,128)(2,1)} %pool.5) | copy-start | bytes 25165828
  29.7 7.5 %copy-start.7 = (s32[1,128,16]{1,2,0:T(8,128)S(1)}, s32[1,128,16]{1,2,0:T(8,128)}, u32[]{:S(2)}) copy-start(s32[1,128,16]{1,2,0:T(8,128)} %param.11) | copy-start | bytes 24580
  35.3 2.0 %copy-start.3 = (bf16[16,4,2,64,256]{4,3,2,1,0:T(8,128)(2,1)}, bf16[16,4,2,64,256]{4,3,2,1,0:T(8,128)(2,1)S(1)}, u32[]{:S(2)}) copy-start(bf16[16,4,2,64,256]{4,3,2,1,0:T(8,128)(2,1)S(1)} %get-tuple-element.16) | copy-start | bytes 12582916
  38.2 29.1 %all-to-all-start.1 = ((bf16[8,2,4096]{2,1,0:T(2,128)(2,1)}), bf16[8,2,4096]{2,1,0:T(2,128)(2,1)S(1)}, u32[]{:S(2)}, u32[]{:S(2)}) async-start(bf16[8,2,4096]{2,1,0:T(2,128)(2,1)} %reshape_reshape.12), calls=%async_computation.1 | async-start | bytes 262144 | tf_op jit(solution)/shard_map/all_to_all | solution.py:208
  42.4 3.4 %copy-start.1 = (bf16[1,2,128,64,256]{4,3,2,1,0:T(8,128)(2,1)S(1)}, bf16[1,2,128,64,256]{4,3,2,1,0:T(8,128)(2,1)}, u32[]{:S(2)}) copy-start(bf16[1,2,128,64,256]{4,3,2,1,0:T(8,128)(2,1)} %pool.5) | copy-start | bytes 25165828
  67.3 53.7 %all-to-all-start.2 = ((bf16[8,2,4,2,64,256]{5,4,3,2,1,0:T(8,128)(2,1)}), bf16[8,2,4,2,64,256]{5,4,3,2,1,0:T(8,128)(2,1)}, u32[]{:S(2)}, u32[]{:S(2)}) async-start(bf16[8,2,4,2,64,256]{5,4,3,2,1,0:T(8,128)(2,1)} %bitcast.97), calls=%async_computation.2 | async-start | bytes 8388608 | tf_op jit(solution)/shard_map/all_to_all | solution.py:205
  71.9 66.4 %reduce-scatter.3.cloned.1.call-start = ((), (), s32[]{:S(2)}) async-start(), calls=%async_computation.5 | async-start | bytes 2621440 | tf_op jit(solution)/shard_map/reduce_scatter | solution.py:264
  88.5 93.2 %reduce-scatter.5.cloned.1.call-start = ((), (), s32[]{:S(2)}) async-start(), calls=%async_computation.6 | async-start | bytes 2621440 | tf_op jit(solution)/shard_map/reduce_scatter | solution.py:264
  88.8 3.4 %copy-start.2 = (bf16[1,2,128,64,256]{4,3,2,1,0:T(8,128)(2,1)S(1)}, bf16[1,2,128,64,256]{4,3,2,1,0:T(8,128)(2,1)}, u32[]{:S(2)}) copy-start(bf16[1,2,128,64,256]{4,3,2,1,0:T(8,128)(2,1)} %pool.5) | copy-start | bytes 25165828
  140.9 40.8 %copy-start.5 = (bf16[32,8192]{1,0:T(8,128)(2,1)S(1)}, bf16[32,8192]{1,0:T(8,128)(2,1)}, u32[]{:S(2)}) copy-start(bf16[32,8192]{1,0:T(8,128)(2,1)} %reduce-scatter.3.cloned.1.call-done) | copy-start | bytes 1572868
Sparse Core Ops, SparseCore 0:
  88.7 45.5 reduce-scatter.2
  138.4 43.2 reduce-scatter.4
